TPU v7x, 512 devices: a whole 4x4x16 slice. The times are simulated.
512 devices in a mesh: grp: 16 (over z_lo, core), seq: 32 (over x, y, z_hi).
Axes of the slice: x: 4, y: 4, z: 16 (z_hi: 2, z_lo: 8; z = z_hi * 8 + z_lo), core: 2. Of those that a mesh axis runs over, the one named last changes fastest.
Arguments:
- latent: float32 [16, 1024, 64], P('grp', 'seq'), may hold values from -6 to 6
- step_noise: float32 [16, 2, 1024, 64], P('grp', None, 'seq'), may hold values from -6 to 6
- start_index: int32 [16], P('grp'), may hold values from 1 to 8
- mod_table: float32 [10, 6144], replicated, may hold values from -3 to 3
- in_weight: bfloat16 [64, 3072], replicated, may hold values from -0.75 to 0.75
- in_bias: float32 [3072], replicated, may hold values from -3 to 3
- base_weight: bfloat16 [3, 32, 1536, 128], P(None, 'seq'), may hold values from -0.109375 to 0.109375
- factor_store: bfloat16 [240, 4096], P('grp'), may hold values from -0.19921875 to 0.19921875
- block_order: int32 [240], replicated, may hold values from 0 to 239, each once
- out_weight: bfloat16 [2048, 64], P('seq'), may hold values from -0.5 to 0.5
Outputs:
- latent_out: float32 [16, 1024, 64], P('grp', 'seq')
- velocity_out: float32 [16, 1024, 64], P('grp', 'seq')
Inputs may be any that keep to these rules, and one draw needn't show every extreme that they name: `block_order`: every logical block is held in exactly one stored row.
All inputs are finite; a program needn't handle non-finite values.
Results may differ from a plain program's by a relative error of at most 0.017.
Values may be sent and summed in bfloat16 or wider, within the bound.
A program may use at most 64 MiB of HBM per device.

v0:
```python
import jax
import jax.numpy as jnp
from jax import lax
from jax.sharding import PartitionSpec as P

D = 3072
HD = 128
RANK = 64
BW = 64
TSTEPS = 10
STEPS = 2


def from_partner(value, axis, apart):
    return lax.ppermute(value, axis, [(i, i ^ 1 << apart) for i in range(lax.axis_size(axis))])


def sigma_at(index):
    remaining = 1.0 - index.astype(jnp.float32) / TSTEPS
    return 3.0 * remaining / (1.0 + 2.0 * remaining)


def plan(index):
    sigma_now = sigma_at(index)
    sigma_step = sigma_at(index + 1) - sigma_now
    spread = 0.7 * jnp.sqrt(sigma_now / (1.0 - sigma_now))
    return (sigma_now, sigma_step, spread)


def modulate(hidden, shift, scaling):
    average = jnp.mean(hidden, axis=-1, keepdims=True)
    centred = hidden - average
    variance = jnp.mean(centred * centred, axis=-1, keepdims=True)
    return (centred * lax.rsqrt(variance + 1e-06) * (1.0 + scaling) + shift).astype(jnp.bfloat16)


def project_rows(gathered, in_weight, in_bias, shift, scaling, merged, row_start):
    row_count = gathered.shape[0]
    block = min(row_count, 512)
    row_total = merged.shape[1]

    def project_one_block(piece):
        hidden = jnp.dot(piece, in_weight, preferred_element_type=jnp.float32) + in_bias
        normed = modulate(hidden, shift, scaling)
        normed_part = lax.dynamic_slice_in_dim(normed, row_start, row_total, 1)
        return jnp.einsum("rd,mdc->mrc", normed_part, merged, preferred_element_type=jnp.float32)

    blocks = lax.map(
        project_one_block, gathered.reshape(row_count // block, block, gathered.shape[1])
    )
    return blocks.transpose(1, 0, 2, 3).reshape(3, row_count, merged.shape[2])


def attend(queries, key_rows, value_rows):
    row_count = queries.shape[0]
    block = min(row_count, 512)

    def attend_one_block(query_block):
        scores = jnp.einsum(
            "qd,kd->qk", query_block, key_rows, preferred_element_type=jnp.float32
        ) * HD ** (-0.5)
        exponent = jnp.exp(scores)
        weights = (exponent / jnp.sum(exponent, axis=-1, keepdims=True)).astype(jnp.bfloat16)
        return jnp.dot(weights, value_rows, preferred_element_type=jnp.float32).astype(jnp.bfloat16)

    blocks = lax.map(attend_one_block, queries.reshape(row_count // block, block, queries.shape[1]))
    return blocks.reshape(row_count, value_rows.shape[1])


def shards(
    latent,
    step_noise,
    start_index,
    mod_table,
    in_weight,
    in_bias,
    base_weight,
    factor_store,
    block_order,
    out_weight,
):
    seq_count = lax.axis_size("seq")
    position = lax.axis_index("seq")
    head_size = base_weight.shape[3]
    half_d = base_weight.shape[2]
    wide = seq_count // 2 * head_size
    pair_bit = position % 2
    head_number = position // 2
    gathered = lax.all_gather(factor_store, "grp", axis=0, tiled=True)
    logical = jnp.zeros_like(gathered).at[block_order].set(gathered)
    stacked = (
        logical.reshape(logical.shape[0], RANK, BW)
        .transpose(1, 0, 2)
        .reshape(RANK, logical.shape[0] * BW)
    )
    span = D + wide
    own_base = base_weight[:, 0]
    row_start = pair_bit * half_d
    row_total = own_base.shape[1]
    merged_list = []
    for member in range(3):
        lower = lax.dynamic_slice_in_dim(stacked, member * span + row_start, row_total, 1)
        upper = lax.dynamic_slice_in_dim(
            stacked, member * span + D + head_number * head_size, head_size, 1
        )
        delta = lax.dot_general(
            lower, upper, (((0,), (0,)), ((), ())), preferred_element_type=jnp.float32
        )
        merged_list.append((own_base[member].astype(jnp.float32) + delta).astype(jnp.bfloat16))
    merged = jnp.stack(merged_list)
    current = latent[0]
    velocity = jnp.zeros_like(current)
    positions = jnp.arange(TSTEPS, dtype=jnp.int32)
    for section in range(STEPS):
        index = start_index[0] + section
        sigma_now, sigma_step, spread = plan(index)
        selector = (positions == index).astype(jnp.float32)
        table_row = jnp.dot(selector, mod_table, precision=lax.Precision.HIGHEST)
        rows_in = lax.all_gather(current.astype(jnp.bfloat16), "seq", axis=0, tiled=True)
        partial_sums = project_rows(
            rows_in, in_weight, in_bias, table_row[:D], table_row[D:], merged, row_start
        )
        partner = from_partner(partial_sums, "seq", 0)
        projected = (partial_sums + partner).astype(jnp.bfloat16)
        attended = attend(projected[0], projected[1], projected[2])
        own_columns = lax.dynamic_slice_in_dim(
            attended, pair_bit * (head_size // 2), head_size // 2, 1
        )
        summand = jnp.dot(own_columns, out_weight, preferred_element_type=jnp.float32)
        velocity = lax.psum_scatter(summand, "seq", scatter_dimension=0, tiled=True)
        current = (
            current * (1.0 + spread * spread / (2.0 * sigma_now) * sigma_step)
            + velocity
            * (1.0 + spread * spread * (1.0 - sigma_now) / (2.0 * sigma_now))
            * sigma_step
            + spread * jnp.sqrt(-sigma_step) * step_noise[0, section]
        )
    return (current[None], velocity[None])


def solution(mesh):
    in_specs = (
        P("grp", "seq", None),
        P("grp", None, "seq", None),
        P("grp"),
        P(),
        P(),
        P(),
        P(None, "seq", None, None),
        P("grp", None),
        P(),
        P("seq", None),
    )
    out_specs = (P("grp", "seq", None), P("grp", "seq", None))
    return jax.shard_map(shards, mesh=mesh, in_specs=in_specs, out_specs=out_specs, check_vma=False)
```

profile of v0, /device:TPU:32, one launch (start us, length us, event | category | flops | bytes accessed | tf_op | source)
XLA Modules:
  0.0 1226.2 jit_solution(5128305180764721769)
XLA Ops:
  7.2 0.7 all-gather.4.cloned.1.call-update
  8.6 0.7 convert_element_type.78
  9.4 167.1 %all-gather = bf16[1,1024,64]{2,1,0:T(8,128)(2,1)S(1)} all-gather(bf16[1,32,64]{2,1,0:T(8,128)(2,1)S(1)} %convert_element_type.78), channel_id=2, replica_groups=mesh['grp'=16,'seq'=32] {'seq'}, dimensions={1}, use_global_device_ids=true | all-gather | bytes 135168 | tf_op jit(solution)/shard_map/all_gather | solution.py:119
  176.5 0.7 compare_select_fusion
  177.2 0.2 fusion.82
  177.5 1.9 reshape.112
  179.4 4.7 scatter_custom_fusion
  184.1 3.2 copy.21
  187.3 3.1 copy.22
  190.5 4.5 reshape.91
  195.0 1.3 fusion.59
  196.3 1.3 fusion.60
  197.6 1.3 fusion.61
  199.0 1.2 pad_maximum_fusion
  200.1 0.1 broadcast.103.clone
  200.3 6.7 while.44
  200.3 1.0 add_reduce_fusion.4
  201.3 1.0 multiply_reduce_fusion.4
  202.4 0.1 dynamic-slice.9
  202.5 0.1 dynamic-slice.8
  202.6 1.0 fusion.124
  203.6 1.0 add_reduce_fusion.4
  204.7 1.0 multiply_reduce_fusion.4
  205.7 0.1 dynamic-slice.9
  205.8 0.1 dynamic-slice.8
  206.0 1.0 fusion.124
  207.0 1.3 copy.23
  208.3 1.9 collective-permute-start
  210.2 130.0 %collective-permute-done = f32[3,1024,128]{2,1,0:T(8,128)S(1)} collective-permute-done((f32[3,1024,128]{2,1,0:T(8,128)}, f32[3,1024,128]{2,1,0:T(8,128)S(1)}, u32[]{:S(2)}, u32[]{:S(2)}) %collective-permute-start) | collective-permute-done | bytes 1572896 | tf_op jit(solution)/shard_map/ppermute | solution.py:15
  340.2 1.6 add_convert_fusion.1
  341.9 2.3 while.45
  341.9 0.5 fusion.127
  342.5 0.6 fusion.128
  343.1 0.5 fusion.127
  343.6 0.6 fusion.128
  344.2 1.1 fusion.66
  345.7 0.2 fusion.80
  346.0 298.7 %reduce-scatter.3.cloned.1.call-done = f32[32,64]{1,0:T(8,128)} async-done(((f32[1024,64]{1,0:T(8,128)}), f32[32,64]{1,0:T(8,128)}) %reduce-scatter.3.cloned.1.call-update) | async-done | bytes 8208 | tf_op jit(solution)/shard_map/reduce_scatter | solution.py:130
  644.7 0.7 fusion.90
  645.4 159.5 %all_gather.11 = bf16[1024,64]{1,0:T(8,128)(2,1)S(1)} all-gather(bf16[32,64]{1,0:T(8,128)(2,1)S(1)} %get-tuple-element.334), channel_id=1, replica_groups=mesh['grp'=16,'seq'=32] {'seq'}, dimensions={0}, use_global_device_ids=true | all-gather | bytes 135168 | tf_op jit(solution)/shard_map/all_gather | solution.py:119
  804.9 0.1 broadcast.103
  805.0 6.7 while.46
  805.0 1.0 add_reduce_fusion.5
  806.1 1.0 multiply_reduce_fusion.5
  807.1 0.1 dynamic-slice.11
  807.2 0.1 dynamic-slice.10
  807.3 1.0 fusion.132
  808.4 1.0 add_reduce_fusion.5
  809.4 1.0 multiply_reduce_fusion.5
  810.5 0.1 dynamic-slice.11
  810.6 0.1 dynamic-slice.10
  810.7 1.0 fusion.132
  811.8 0.1 copy.24
  811.9 13.5 %collective-permute-start.1 = (f32[3,1024,128]{2,1,0:T(8,128)S(1)}, f32[3,1024,128]{2,1,0:T(8,128)S(1)}, u32[]{:S(2)}, u32[]{:S(2)}) collective-permute-start(f32[3,1024,128]{2,1,0:T(8,128)S(1)} %bitcast.172), channel_id=1, source_target_pairs={{0,1},{1,0},{2,3},{3,2},{4,5},{5,4},{6,7},{7,6},{8,9},{9,8},{10,11... | collective-permute-start | bytes 4718600 | tf_op jit(solution)/shard_map/ppermute | solution.py:15
  825.3 61.8 %collective-permute-done.1 = f32[3,1024,128]{2,1,0:T(8,128)S(1)} collective-permute-done((f32[3,1024,128]{2,1,0:T(8,128)S(1)}, f32[3,1024,128]{2,1,0:T(8,128)S(1)}, u32[]{:S(2)}, u32[]{:S(2)}) %collective-permute-start.1) | collective-permute-done | bytes 1572896 | tf_op jit(solution)/shard_map/ppermute | solution.py:15
  887.1 0.2 add_convert_fusion
  887.4 2.3 while.47
  887.4 0.5 fusion.135
  888.0 0.6 fusion.136
  888.6 0.5 fusion.135
  889.1 0.6 fusion.136
  889.7 1.1 fusion.64
  891.1 327.3 %reduce-scatter.5.cloned.1.call-done = f32[32,64]{1,0:T(8,128)} async-done(((f32[1024,64]{1,0:T(8,128)}), f32[32,64]{1,0:T(8,128)}) %reduce-scatter.5.cloned.1.call-update) | async-done | bytes 8208 | tf_op jit(solution)/shard_map/reduce_scatter | solution.py:130
  1218.4 1.3 fusion.71
  (44 shorter events, 0.7 us)
Async XLA Ops:
  7.2 170.0 %copy-start = (f32[10,6144]{1,0:T(8,128)S(1)}, f32[10,6144]{1,0:T(8,128)}, u32[]{:S(2)}) copy-start(f32[10,6144]{1,0:T(8,128)} %param.21) | copy-start | bytes 737284
  7.2 170.3 %all-gather.4.cloned.1.call-start = ((), (), s32[]{:S(2)}) async-start(), calls=%async_computation.4 | async-start | bytes 2228224 | tf_op jit(solution)/shard_map/all_gather | solution.py:89
  7.9 636.8 %reduce-scatter.3.cloned.1.call-start = ((), (), s32[]{:S(2)}) async-start(), calls=%async_computation.2 | async-start | bytes 540672 | tf_op jit(solution)/shard_map/reduce_scatter | solution.py:130
  198.9 1.3 copy-start.1
  199.0 1.3 copy-start.2
  201.3 1.3 copy-start.3
  204.7 1.3 copy-start.3
  208.3 131.9 %collective-permute-start = (f32[3,1024,128]{2,1,0:T(8,128)}, f32[3,1024,128]{2,1,0:T(8,128)S(1)}, u32[]{:S(2)}, u32[]{:S(2)}) collective-permute-start(f32[3,1024,128]{2,1,0:T(8,128)} %bitcast.27), channel_id=1, source_target_pairs={{0,1},{1,0},{2,3},{3,2},{4,5},{5,4},{6,7},{7,6},{8,9},{9,8},{10,11... | collective-permute-start | bytes 4718600 | tf_op jit(solution)/shard_map/ppermute | solution.py:15
  341.9 2.3 copy-start.5
  341.9 302.8 %copy-start.6 = (f32[1,32,64]{2,1,0:T(8,128)S(1)}, f32[1,32,64]{2,1,0:T(8,128)}, u32[]{:S(2)}) copy-start(f32[1,32,64]{2,1,0:T(8,128)} %param.18) | copy-start | bytes 24580
  341.9 302.8 %copy-start.7 = (f32[1,2,32,64]{3,2,1,0:T(8,128)S(1)}, f32[1,2,32,64]{3,2,1,0:T(8,128)}, u32[]{:S(2)}) copy-start(f32[1,2,32,64]{3,2,1,0:T(8,128)} %param.19) | copy-start | bytes 49156
  345.3 873.0 %reduce-scatter.5.cloned.1.call-start = ((), (), s32[]{:S(2)}) async-start(), calls=%async_computation.3 | async-start | bytes 540672 | tf_op jit(solution)/shard_map/reduce_scatter | solution.py:130
  806.1 1.3 copy-start.4
  809.4 1.3 copy-start.4
  811.9 75.3 %collective-permute-start.1 = (f32[3,1024,128]{2,1,0:T(8,128)S(1)}, f32[3,1024,128]{2,1,0:T(8,128)S(1)}, u32[]{:S(2)}, u32[]{:S(2)}) collective-permute-start(f32[3,1024,128]{2,1,0:T(8,128)S(1)} %bitcast.172), channel_id=1, source_target_pairs={{0,1},{1,0},{2,3},{3,2},{4,5},{5,4},{6,7},{7,6},{8,9},{9,8},{10,11... | collective-permute-start | bytes 4718600 | tf_op jit(solution)/shard_map/ppermute | solution.py:15
Sparse Core Ops, SparseCore 0:
  10.1 99.5 all-gather.3
  345.5 299.1 reduce-scatter.2
  890.9 327.4 reduce-scatter.4
where the time goes:
time: 1230 us
  waiting for transfers between devices  819 us (67%)
  blocking collectives  327 us (27%)
  local copies, waits for them, and re-layouts  20.2 us (2%)
  matrix products  19.3 us (2%)
  starting transfers between devices  15.5 us (1%)
  between operations  15.3 us (1%)
    reduce_scatter x2, waiting for transfers between devices, shards(): velocity = lax.psum_scatter(summand, 'seq', scatter_dimension=0, tiled=True)  626 us
    all_gather x2, blocking collectives, shards(): lax.all_gather(current.astype(jnp.bfloat16), 'seq', axis=0, tiled=True)  327 us
    ppermute x2, waiting for transfers between devices, from_partner(): lax.ppermute(value, axis, [(i, i ^ 1 << apart) for i in range(lax.axis_si...  192 us
  transfers between devices with their start and end apart: 5, of which 4 were waited for; matrix products, arithmetic and copies ran while one was open for 0% of the time, Pallas kernels for 0%

commit v1 on v0

v1 whole, which is shorter than its diff:
```python
import functools
import math

import jax
import jax.numpy as jnp
from jax import lax
from jax.experimental import pallas as pl
from jax.experimental.pallas import tpu as pltpu
from jax.sharding import PartitionSpec as P

D = 3072
C = 64
HD = 128
RANK = 64
BW = 64
TSTEPS = 10
STEPS = 2
MESH = pl.DeviceIdType.MESH
F32 = jnp.float32
BF16 = jnp.bfloat16
ROWS = 80
NT = (((1,), (1,)), ((), ()))


def dot(a, b, dims=(((1,), (0,)), ((), ()))):
    return lax.dot_general(a, b, dims, preferred_element_type=F32)


def exact_dot(a, b, dims=(((1,), (0,)), ((), ()))):
    return lax.dot_general(
        a, b, dims, preferred_element_type=F32, precision=lax.Precision.HIGHEST
    )


def sigma_at(index):
    remaining = 1.0 - index.astype(F32) / TSTEPS
    return 3.0 * remaining / (1.0 + 2.0 * remaining)


def plan(index):
    sigma_now = sigma_at(index)
    sigma_step = sigma_at(index + 1) - sigma_now
    spread = 0.7 * jnp.sqrt(sigma_now / (1.0 - sigma_now))
    return (sigma_now, sigma_step, spread)


def advance(state, velocity, noise, index):
    sigma_now, sigma_step, spread = plan(jnp.full(state.shape, index, jnp.int32))
    return (
        state * (1.0 + spread * spread / (2.0 * sigma_now) * sigma_step)
        + velocity * (1.0 + spread * spread * (1.0 - sigma_now) / (2.0 * sigma_now)) * sigma_step
        + spread * jnp.sqrt(-sigma_step) * noise
    )


def token_features(state, in_weight, in_bias):
    latent_in = state.astype(BF16)
    hidden = dot(latent_in, in_weight) + in_bias
    average = jnp.mean(hidden, axis=-1, keepdims=True)
    centred = hidden - average
    variance = jnp.mean(centred * centred, axis=-1, keepdims=True)
    scale = lax.rsqrt(variance + 1e-06)
    scaled = latent_in.astype(F32) * scale
    high = scale.astype(BF16).astype(F32)
    lane = lax.broadcasted_iota(jnp.int32, scaled.shape, 1)
    rest = jnp.where(
        lane == 0, high, jnp.where(lane == 1, 1.0, jnp.where(lane == 2, scale - high, 0.0))
    )
    return jnp.concatenate([scaled, rest], axis=1).astype(BF16)


def attend(queries, tokens, score_map):
    mapped = dot(queries, score_map).astype(BF16)
    exponent = jnp.exp2(dot(mapped, tokens, NT))
    weights = (exponent / jnp.sum(exponent, axis=-1, keepdims=True)).astype(BF16)
    return dot(weights, tokens).astype(BF16)


def kernel(
    groups, heads,
    start_ref, latent_ref, noise_ref, mod_hbm, win_hbm, bias_ref, base_hbm, fac_ref, order_ref, wout_ref,
    latent_out, velocity_out,
    mod, win, base, state, noise0, wout, store, perm_even, perm_odd, folded,
    own_part, part_out, part_in, rank_out, rank_in, tokens, vel_out0, vel_in0, vel_out1, vel_in1,
    load_sem, col_send, col_recv, pair_send, pair_recv, plane_send, plane_recv,
):
    g = lax.axis_index("grp")
    s = lax.axis_index("seq")
    core, zlo = g % 2, g // 2
    zcount = groups // 2
    head, half = s // 2, s % 2
    own = latent_ref.shape[1]
    both = 2 * own
    half_d = D // 2
    store_rows = fac_ref.shape[0]
    block_rows = store.shape[2]
    pairs = D // 128
    per_member = 2 * (pairs + heads)

    def column(i):
        return ((zlo + i) % zcount * 2 + core, s)

    sibling = (g + 1 - 2 * core, s)
    partner = (g, s + 1 - 2 * half)

    def plane(h):
        return (g, h * 2 + half)

    loads = [
        pltpu.make_async_copy(src, dst, load_sem.at[i])
        for i, (src, dst) in enumerate([(win_hbm, win), (mod_hbm, mod), (base_hbm, base)])
    ]
    for load in loads:
        load.start()

    barrier = pltpu.get_barrier_semaphore()

    def greet(device):
        pl.semaphore_signal(barrier, inc=1, device_id=device, device_id_type=MESH)

    def greet_column(i, carry):
        greet(column(i))
        return carry

    def greet_plane(i, carry):
        greet(plane((head + i) % heads))
        return carry

    lax.fori_loop(1, zcount, greet_column, 0)
    greet(sibling)
    greet(partner)
    lax.fori_loop(1, heads, greet_plane, 0)

    store[core, zlo] = jnp.zeros(store.shape[2:], BF16)
    lanes = pl.ds(pl.multiple_of(head * 256, 256), 256)
    store[core, zlo, :store_rows, :] = fac_ref[:, lanes]
    own_rows = pl.ds(pl.multiple_of(half * own, own), own)
    state[own_rows, :] = latent_ref[0]
    noise0[own_rows, :] = noise_ref[0, 0]
    wout_rows = pl.ds(pl.multiple_of(half * 64, 64), 64)
    wout[wout_rows, :] = wout_ref[...]

    pl.semaphore_wait(barrier, zcount - 1 + 2 + heads - 1)

    def column_copy(i):
        place = store.at[core, zlo]
        return pltpu.make_async_remote_copy(
            src_ref=place, dst_ref=place,
            send_sem=col_send.at[i], recv_sem=col_recv.at[zlo],
            device_id=column(i), device_id_type=MESH,
        )

    def column_arrival(i):
        other = (zlo + i) % zcount
        place = store.at[core, other]
        return pltpu.make_async_remote_copy(
            src_ref=place, dst_ref=place,
            send_sem=col_send.at[i], recv_sem=col_recv.at[other],
            device_id=column(i), device_id_type=MESH,
        )

    def pair_copy(i, src, dst):
        return pltpu.make_async_remote_copy(
            src_ref=src, dst_ref=dst,
            send_sem=pair_send.at[i], recv_sem=pair_recv.at[i],
            device_id=partner, device_id_type=MESH,
        )

    def start_column(i, carry):
        column_copy(i).start()
        return carry

    lax.fori_loop(1, zcount, start_column, 0)
    pair_copies = [
        pair_copy(0, state.at[own_rows], state.at[own_rows]),
        pair_copy(1, noise0.at[own_rows], noise0.at[own_rows]),
        pair_copy(2, wout.at[wout_rows], wout.at[wout_rows]),
    ]
    other_rows = pl.ds(pl.multiple_of((1 - half) * own, own), own)
    other_wout = pl.ds(pl.multiple_of((1 - half) * 64, 64), 64)
    pair_arrivals = [
        pair_copy(0, state.at[other_rows], state.at[other_rows]),
        pair_copy(1, noise0.at[other_rows], noise0.at[other_rows]),
        pair_copy(2, wout.at[other_wout], wout.at[other_wout]),
    ]
    for copy in pair_copies:
        copy.start()

    start = start_ref[0]
    loads[0].wait()
    loads[1].wait()
    in_weight = win[...].astype(F32)
    in_bias = bias_ref[...]
    weight_centred = in_weight - jnp.mean(in_weight, axis=-1, keepdims=True)
    bias_centred = in_bias - jnp.mean(in_bias, axis=-1, keepdims=True)
    extra_row = lax.broadcasted_iota(jnp.int32, (16, D), 0)
    for step in range(STEPS):
        shift = mod[pl.ds(start + step, 1), :D]
        gain = 1.0 + mod[pl.ds(start + step, 1), D:]
        folded[step, :64, :] = (weight_centred * gain).astype(BF16)
        is_bias = (extra_row == 0) | (extra_row == 2)
        extra = jnp.where(is_bias, bias_centred * gain, jnp.where(extra_row == 1, shift, 0.0))
        folded[step, 64:80, :] = extra.astype(BF16)
        folded[step, 80:, :] = jnp.zeros((48, D), BF16)

    loads[2].wait()
    half_lanes = pl.ds(pl.multiple_of(half * half_d, 128), half_d)
    part_copies = []
    for step in range(STEPS):
        left = folded[step, :, half_lanes]
        for member in range(3):
            part = dot(left, base[member, 0])
            own_part[step, :, member * HD:(member + 1) * HD] = part
            part_out[step, :, member * HD:(member + 1) * HD] = part[:ROWS].astype(BF16)
        part_copies.append(pair_copy(3 + step, part_out.at[step], part_in.at[step]))
        part_copies[-1].start()

    for copy in pair_arrivals:
        copy.wait_recv()
    in_weight_bf = win[...]
    tokens[0, head] = token_features(state[...], in_weight_bf, in_bias)

    def plane_copy(kind, src, dst, peer):
        return pltpu.make_async_remote_copy(
            src_ref=src, dst_ref=dst,
            send_sem=plane_send.at[kind, peer], recv_sem=plane_recv.at[kind, head],
            device_id=plane(peer), device_id_type=MESH,
        )

    def plane_arrival(kind, buffer, peer):
        return pltpu.make_async_remote_copy(
            src_ref=buffer.at[peer], dst_ref=buffer.at[peer],
            send_sem=plane_send.at[kind, peer], recv_sem=plane_recv.at[kind, peer],
            device_id=plane(peer), device_id_type=MESH,
        )

    def send_plane(kind, src_of, dst):
        def body(i, carry):
            peer = (head + i) % heads
            plane_copy(kind, src_of(peer), dst.at[head], peer).start()
            return carry

        lax.fori_loop(1, heads, body, 0)

    def receive_plane(kind, buffer):
        def body(i, carry):
            plane_arrival(kind, buffer, (head + heads - i) % heads).wait_recv()
            return carry

        lax.fori_loop(1, heads, body, 0)

    def finish_plane(kind, buffer):
        def body(i, carry):
            plane_arrival(kind, buffer, (head + i) % heads).wait_send()
            return carry

        lax.fori_loop(1, heads, body, 0)

    send_plane(1, lambda peer: tokens.at[0, head], tokens.at[0])

    stored = zcount * 2 * store_rows
    row = lax.broadcasted_iota(jnp.int32, (stored, 256), 0)
    col = lax.broadcasted_iota(jnp.int32, (stored, 256), 1)
    in_block = col % block_rows
    slot = col // block_rows
    shard = slot % zcount * 2 + slot // zcount
    source = jnp.where(in_block < store_rows, shard * store_rows + in_block, -1)
    place = (row == source).astype(F32).astype(BF16)
    order = jnp.broadcast_to((order_ref[...] + 1).astype(F32), (16, stored)).astype(BF16)
    order = dot(order, place)[0:1].astype(jnp.int32) - 1
    total = (pairs + heads) * 16
    line = lax.broadcasted_iota(jnp.int32, (total, 256), 0)
    entry = line & 15
    member_of = entry - 3 * ((entry * 11) >> 5)
    target = jnp.where(entry < 12, member_of * per_member + 2 * (line >> 4), -8)
    perm_even[...] = (target == order).astype(F32).astype(BF16)
    perm_odd[...] = (target + 1 == order).astype(F32).astype(BF16)

    def wait_column(i, carry):
        column_arrival(zcount - i).wait_recv()
        return carry

    lax.fori_loop(1, zcount, wait_column, 0)
    to_sibling = pltpu.make_async_remote_copy(
        src_ref=store.at[core], dst_ref=store.at[core],
        send_sem=pair_send.at[5], recv_sem=pair_recv.at[5],
        device_id=sibling, device_id_type=MESH,
    )
    to_sibling.start()
    from_sibling = pltpu.make_async_remote_copy(
        src_ref=store.at[1 - core], dst_ref=store.at[1 - core],
        send_sem=pair_send.at[5], recv_sem=pair_recv.at[5],
        device_id=sibling, device_id_type=MESH,
    )
    from_sibling.wait_recv()
    blocks = store[...].reshape(256, 256)
    even = dot(perm_even[...], blocks)
    odd = dot(perm_odd[...], blocks)
    lane = lax.broadcasted_iota(jnp.int32, (total, 128), 1)
    entry = lax.broadcasted_iota(jnp.int32, (total, 128), 0) & 15
    rank = (entry * 11) >> 5
    even = jnp.where(rank < 2, even[:, :128], even[:, 128:])
    odd = jnp.where(rank < 2, odd[:, :128], odd[:, 128:])
    first = (rank & 1) == 0
    spread = jnp.where(
        lane < 64,
        jnp.where(first, even, pltpu.roll(even, 64, 1)),
        jnp.where(first, pltpu.roll(odd, 64, 1), odd),
    ).astype(BF16)
    lower = jnp.concatenate([spread[i * 16:(i + 1) * 16] for i in range(pairs)], axis=1)
    inner = [dot(lower, folded[step], NT).astype(BF16) for step in range(STEPS)]
    for other in range(heads):
        rank_out[other, :, 0:128] = inner[0]
        rank_out[other, :, 128:256] = inner[1]
        rank_out[other, :, 256:384] = spread[(pairs + other) * 16:(pairs + other + 1) * 16]
    rank_in[head] = rank_out[head]
    send_plane(0, lambda peer: rank_out.at[peer], rank_in)
    receive_plane(0, rank_in)
    for step in range(STEPS):
        pair_copy(3 + step, part_out.at[step], part_in.at[step]).wait_recv()
    ranks = rank_in[...].reshape(heads * 16, 384)
    entry = lax.broadcasted_iota(jnp.int32, (heads * 16, HD), 0) & 15
    member_of = entry - 3 * ((entry * 11) >> 5)
    upper = ranks[:, 256:].astype(F32)
    upper = jnp.concatenate(
        [jnp.where(member_of == member, upper, 0.0) for member in range(3)], axis=1
    ).astype(BF16)
    low_rank = dot(ranks[:, :256].astype(F32).T.astype(BF16), upper)
    out_weight = wout[...].astype(F32)
    score_maps, value_maps = [], []
    for step in range(STEPS):
        received = jnp.concatenate(
            [part_in[step].astype(F32), jnp.zeros((128 - ROWS, 3 * HD), F32)], axis=0
        )
        full = own_part[step] + received + low_rank[step * 128:(step + 1) * 128]
        score_map = exact_dot(full[:, :HD], full[:, HD:2 * HD], NT)
        score_maps.append((score_map * (HD ** (-0.5) * math.log2(math.e))).astype(BF16))
        value_map = exact_dot(full[:, 2 * HD:], out_weight)
        nothing = jnp.zeros_like(value_map)
        value_maps.append(
            jnp.concatenate(
                [
                    jnp.concatenate([value_map, nothing], axis=1),
                    jnp.concatenate([nothing, value_map], axis=1),
                ],
                axis=0,
            ).astype(BF16)
        )

    owners = 4
    receive_plane(1, tokens.at[0])
    keys = tokens[0].reshape(heads * both, 128)
    for part in range(heads // owners):
        first_owner = (head // owners + part) % (heads // owners) * owners
        queries = tokens[0, pl.ds(first_owner, owners)].reshape(owners * both, 128)
        attended = attend(queries, keys, score_maps[0]).reshape(owners, both, 128)
        sides = jnp.concatenate(
            [
                attended[:, :own].reshape(owners * own, 128),
                attended[:, own:].reshape(owners * own, 128),
            ],
            axis=1,
        )
        velocity = dot(sides, value_maps[0]).astype(BF16).reshape(owners, own, 128)
        vel_out0[pl.ds(first_owner, owners)] = velocity
        for i in range(owners):
            peer = first_owner + i

            @pl.when(peer != head)
            def _():
                plane_copy(2, vel_out0.at[peer], vel_in0.at[head], peer).start()

    vel_in0[head] = vel_out0[head]
    pair_copies[0].wait_send()
    receive_plane(2, vel_in0)
    velocity = jnp.sum(vel_in0[...].astype(F32), axis=0)
    velocity = jnp.concatenate([velocity[:, :C], velocity[:, C:]], axis=0)
    state[...] = advance(state[...], velocity, noise0[...], start)
    tokens[1, head] = token_features(state[...], in_weight_bf, in_bias)
    send_plane(3, lambda peer: tokens.at[1, head], tokens.at[1])
    receive_plane(3, tokens.at[1])

    owners = 8
    keys = tokens[1].reshape(heads * both, 128)
    quarter = own // 2
    for part in range(heads // owners):
        first_owner = (head // owners + part) % (heads // owners) * owners
        queries = tokens[1, pl.ds(first_owner, owners), own_rows, :].reshape(owners * own, 128)
        attended = attend(queries, keys, score_maps[1]).reshape(owners, own, 128)
        sides = jnp.concatenate(
            [
                attended[:, :quarter].reshape(owners * quarter, 128),
                attended[:, quarter:].reshape(owners * quarter, 128),
            ],
            axis=1,
        )
        velocity = dot(sides, value_maps[1]).astype(BF16).reshape(owners, quarter, 128)
        vel_out1[pl.ds(first_owner, owners)] = velocity
        for i in range(owners):
            peer = first_owner + i

            @pl.when(peer != head)
            def _():
                plane_copy(4, vel_out1.at[peer], vel_in1.at[head], peer).start()

    vel_in1[head] = vel_out1[head]
    receive_plane(4, vel_in1)
    velocity = jnp.sum(vel_in1[...].astype(F32), axis=0)
    velocity = jnp.concatenate([velocity[:, :C], velocity[:, C:]], axis=0)
    latent_out[0] = advance(state[own_rows, :], velocity, noise_ref[0, 1], start + 1)
    velocity_out[0] = velocity

    def finish_column(i, carry):
        column_copy(i).wait_send()
        return carry

    lax.fori_loop(1, zcount, finish_column, 0)
    to_sibling.wait_send()
    for copy in pair_copies[1:] + part_copies:
        copy.wait_send()
    finish_plane(0, rank_in)
    finish_plane(1, tokens.at[0])
    finish_plane(2, vel_in0)
    finish_plane(3, tokens.at[1])
    finish_plane(4, vel_in1)


def shards(groups, heads):
    def run(
        latent, step_noise, start_index, mod_table, in_weight, in_bias,
        base_weight, factor_store, block_order, out_weight,
    ):
        own = latent.shape[1]
        block_rows = (factor_store.shape[0] + 15) // 16 * 16
        total = (D // 128 + heads) * 16
        vmem = pl.BlockSpec(memory_space=pltpu.VMEM)
        anywhere = pl.BlockSpec(memory_space=pl.ANY)
        return pl.pallas_call(
            functools.partial(kernel, groups, heads),
            out_shape=(
                jax.ShapeDtypeStruct(latent.shape, F32),
                jax.ShapeDtypeStruct(latent.shape, F32),
            ),
            in_specs=[
                pl.BlockSpec(memory_space=pltpu.SMEM),
                vmem, vmem, anywhere, anywhere, vmem, anywhere, vmem, vmem, vmem,
            ],
            out_specs=(vmem, vmem),
            scratch_shapes=[
                pltpu.VMEM(mod_table.shape, F32),
                pltpu.VMEM(in_weight.shape, BF16),
                pltpu.VMEM(base_weight.shape, BF16),
                pltpu.VMEM((2 * own, C), F32),
                pltpu.VMEM((2 * own, C), F32),
                pltpu.VMEM((HD, C), BF16),
                pltpu.VMEM((2, groups // 2, block_rows, 256), BF16),
                pltpu.VMEM((total, 256), BF16),
                pltpu.VMEM((total, 256), BF16),
                pltpu.VMEM((STEPS, 128, D), BF16),
                pltpu.VMEM((STEPS, 128, 3 * HD), F32),
                pltpu.VMEM((STEPS, ROWS, 3 * HD), BF16),
                pltpu.VMEM((STEPS, ROWS, 3 * HD), BF16),
                pltpu.VMEM((heads, 16, 384), BF16),
                pltpu.VMEM((heads, 16, 384), BF16),
                pltpu.VMEM((STEPS, heads, 2 * own, 128), BF16),
                pltpu.VMEM((heads, own, 128), BF16),
                pltpu.VMEM((heads, own, 128), BF16),
                pltpu.VMEM((heads, own // 2, 128), BF16),
                pltpu.VMEM((heads, own // 2, 128), BF16),
                pltpu.SemaphoreType.DMA((3,)),
                pltpu.SemaphoreType.DMA((max(groups // 2, 2),)),
                pltpu.SemaphoreType.DMA((max(groups // 2, 2),)),
                pltpu.SemaphoreType.DMA((6,)),
                pltpu.SemaphoreType.DMA((6,)),
                pltpu.SemaphoreType.DMA((5, heads)),
                pltpu.SemaphoreType.DMA((5, heads)),
            ],
            compiler_params=pltpu.CompilerParams(
                collective_id=0, has_side_effects=True, vmem_limit_bytes=48 * 1024 * 1024
            ),
        )(
            start_index, latent, step_noise, mod_table, in_weight, in_bias.reshape(1, -1),
            base_weight, factor_store, block_order.reshape(1, -1), out_weight,
        )

    return run


def solution(mesh):
    in_specs = (
        P("grp", "seq", None),
        P("grp", None, "seq", None),
        P("grp"),
        P(),
        P(),
        P(),
        P(None, "seq", None, None),
        P("grp", None),
        P(),
        P("seq", None),
    )
    out_specs = (P("grp", "seq", None), P("grp", "seq", None))
    run = shards(mesh.shape["grp"], mesh.shape["seq"] // 2)
    return jax.shard_map(run, mesh=mesh, in_specs=in_specs, out_specs=out_specs, check_vma=False)
```

time: 1230 us -> 78 us (0.06)
  the two profiles are of different devices: /device:TPU:32 before, /device:TPU:64 now
where the time goes in v1:
time: 78 us; the launch traced here: 77.5 us
  Pallas kernels  67.3 us (86%)
  local copies, waits for them, and re-layouts  8.95 us (11%)
  between operations  1.3 us (2%)
    pallas_call x1, Pallas kernels, run(): pl.pallas_call(functools.partial(kernel, groups, heads), out_shape=(jax.S...  67.3 us
    unnamed x20, local copies, waits for them, and re-layouts  8.95 us

profile of v1, /device:TPU:64, one launch (start us, length us, event | category | flops | bytes accessed | tf_op | source)
XLA Modules:
  0.0 77.5 jit_solution(5351292841334090145)
XLA Ops:
  1.3 0.0 copy-start
  1.3 1.3 %copy-done = bf16[3,1,1536,128]{3,2,1,0:T(8,128)(2,1)S(1)} copy-done((bf16[3,1,1536,128]{3,2,1,0:T(8,128)(2,1)S(1)}, bf16[3,1,1536,128]{3,2,1,0:T(8,128)(2,1)}, u32[]{:S(2)}) %copy-start) | copy-done | bytes 1179672
  2.6 0.0 copy-start.1
  2.6 1.0 %copy-done.1 = f32[10,6144]{1,0:T(8,128)S(1)} copy-done((f32[10,6144]{1,0:T(8,128)S(1)}, f32[10,6144]{1,0:T(8,128)}, u32[]{:S(2)}) %copy-start.1) | copy-done | bytes 245784
  3.5 0.0 copy-start.2
  3.5 1.0 %copy-done.2 = bf16[64,3072]{1,0:T(8,128)(2,1)S(1)} copy-done((bf16[64,3072]{1,0:T(8,128)(2,1)S(1)}, bf16[64,3072]{1,0:T(8,128)(2,1)}, u32[]{:S(2)}) %copy-start.2) | copy-done | bytes 393240
  4.5 0.0 copy-start.3
  4.5 0.9 %copy-done.3 = bf16[15,4096]{1,0:T(8,128)(2,1)S(1)} copy-done((bf16[15,4096]{1,0:T(8,128)(2,1)S(1)}, bf16[15,4096]{1,0:T(8,128)(2,1)}, u32[]{:S(2)}) %copy-start.3) | copy-done | bytes 122904
  5.4 0.0 copy-start.4
  5.5 0.8 copy-done.4
  6.2 0.0 copy-start.5
  6.2 0.7 copy-done.5
  6.9 0.0 copy-start.6
  6.9 0.7 copy-done.6
  7.6 0.0 copy-start.7
  7.6 0.7 copy-done.7
  8.3 0.0 copy-start.8
  8.4 0.7 copy-done.8
  9.0 67.3 %shard_map.113 = (f32[1,32,64]{2,1,0:T(8,128)S(1)}, f32[1,32,64]{2,1,0:T(8,128)S(1)}) custom-call(s32[1]{0:T(128)S(6)} %copy.14.start_ref, f32[1,32,64]{2,1,0:T(8,128)S(1)} %copy-done.5, f32[1,2,32,64]{3,2,1,0:T(8,128)S(1)} %copy-done.4, f32[10,6144]{1,0:T(8,128)S(1)} %copy-done.1, bf16[64,3072]{1,0:T(8,128)(2,1)S(1)} %copy-done.2, f32[1,3072]{1,0:T(1,128)S(1)} %bitcast.2, ...), custom_call_target="tpu_custom_call" | custom-call | tf_op jit(solution)/shard_map/pallas_call | solution.py:438
  76.3 0.6 copy.15
  76.9 0.6 copy.16
Async XLA Ops:
  1.3 1.3 %copy-start = (bf16[3,1,1536,128]{3,2,1,0:T(8,128)(2,1)S(1)}, bf16[3,1,1536,128]{3,2,1,0:T(8,128)(2,1)}, u32[]{:S(2)}) copy-start(bf16[3,1,1536,128]{3,2,1,0:T(8,128)(2,1)} %base_hbm.1) | copy-start | bytes 3538948
  2.6 1.0 %copy-start.1 = (f32[10,6144]{1,0:T(8,128)S(1)}, f32[10,6144]{1,0:T(8,128)}, u32[]{:S(2)}) copy-start(f32[10,6144]{1,0:T(8,128)} %mod_hbm.1) | copy-start | bytes 737284
  3.5 1.0 %copy-start.2 = (bf16[64,3072]{1,0:T(8,128)(2,1)S(1)}, bf16[64,3072]{1,0:T(8,128)(2,1)}, u32[]{:S(2)}) copy-start(bf16[64,3072]{1,0:T(8,128)(2,1)} %win_hbm.1) | copy-start | bytes 1179652
  4.5 0.9 %copy-start.3 = (bf16[15,4096]{1,0:T(8,128)(2,1)S(1)}, bf16[15,4096]{1,0:T(8,128)(2,1)}, u32[]{:S(2)}) copy-start(bf16[15,4096]{1,0:T(8,128)(2,1)} %fac_ref.1) | copy-start | bytes 368644
  5.4 0.8 copy-start.4
  6.2 0.7 copy-start.5
  6.9 0.7 copy-start.6
  7.6 0.7 copy-start.7
  8.3 0.7 copy-start.8

commit v2 on v1

v2 whole, which is shorter than its diff:
```python
import functools
import math

import jax
import jax.numpy as jnp
from jax import lax
from jax.experimental import pallas as pl
from jax.experimental.pallas import tpu as pltpu
from jax.sharding import PartitionSpec as P

D = 3072
C = 64
HD = 128
RANK = 64
BW = 64
TSTEPS = 10
STEPS = 2
MESH = pl.DeviceIdType.MESH
F32 = jnp.float32
BF16 = jnp.bfloat16
QUERY = 64
KEY = 80
ROWS = 80
MAP_ROWS = 96
NT = (((1,), (1,)), ((), ()))
SIDE = 4
OFFSETS = (
    (2, 2), (2, 1), (2, 3), (1, 2), (3, 2), (1, 1), (3, 3), (1, 3), (3, 1),
    (2, 0), (0, 2), (1, 0), (3, 0), (0, 1), (0, 3),
)


def dot(a, b, dims=(((1,), (0,)), ((), ()))):
    return lax.dot_general(a, b, dims, preferred_element_type=F32)


def exact_dot(a, b, dims=(((1,), (0,)), ((), ()))):
    return lax.dot_general(
        a, b, dims, preferred_element_type=F32, precision=lax.Precision.HIGHEST
    )


def sigma_at(index):
    remaining = 1.0 - index.astype(F32) / TSTEPS
    return 3.0 * remaining / (1.0 + 2.0 * remaining)


def plan(index):
    sigma_now = sigma_at(index)
    sigma_step = sigma_at(index + 1) - sigma_now
    spread = 0.7 * jnp.sqrt(sigma_now / (1.0 - sigma_now))
    return (sigma_now, sigma_step, spread)


def advance(state, velocity, noise, index):
    sigma_now, sigma_step, spread = plan(jnp.full(state.shape, index, jnp.int32))
    return (
        state * (1.0 + spread * spread / (2.0 * sigma_now) * sigma_step)
        + velocity * (1.0 + spread * spread * (1.0 - sigma_now) / (2.0 * sigma_now)) * sigma_step
        + spread * jnp.sqrt(-sigma_step) * noise
    )


def token_features(state, in_weight, in_bias):
    latent_in = state.astype(BF16)
    hidden = dot(latent_in, in_weight) + in_bias
    average = jnp.mean(hidden, axis=-1, keepdims=True)
    centred = hidden - average
    variance = jnp.mean(centred * centred, axis=-1, keepdims=True)
    scale = lax.rsqrt(variance + 1e-06)
    scaled = latent_in.astype(F32) * scale
    high = scale.astype(BF16).astype(F32)
    lane = lax.broadcasted_iota(jnp.int32, scaled.shape, 1)
    entry = jnp.where(lane < 2 * (KEY - QUERY), lane & (KEY - QUERY - 1), 3)
    rest = jnp.where(
        entry == 0, high, jnp.where(entry == 1, 1.0, jnp.where(entry == 2, scale - high, 0.0))
    )
    return jnp.concatenate([scaled, rest], axis=1).astype(BF16)


def kernel(
    groups, heads,
    start_ref, latent_hbm, noise_hbm, mod_hbm, win_hbm, bias_hbm, base_hbm, fac_hbm, order_hbm, wout_hbm,
    latent_out, velocity_out,
    mod, win, bias_ref, base, fac_ref, order_ref, latent0, noise0, noise1, wout_half,
    pair_state, wout, store, perm_even, perm_odd, folded,
    own_part, part_out, part_in, rank_out, rank_in, tokens, maps_out, maps_in,
    load_sem, col_send, col_recv, pair_send, pair_recv, plane_send, plane_recv, ready,
):
    g = lax.axis_index("grp")
    s = lax.axis_index("seq")
    core, zlo = g % 2, g // 2
    zcount = groups // 2
    head, half = s // 2, s % 2
    own = latent_hbm.shape[1]
    both = 2 * own
    half_d = D // 2
    store_rows = fac_hbm.shape[0]
    block_rows = store.shape[2]
    pairs = D // 128
    per_member = 2 * (pairs + heads)

    sibling = (g + 1 - 2 * core, s)
    partner = (g, s + 1 - 2 * half)

    def column_target(j):
        return jnp.where(zlo < zcount // 2, zcount - 1 - j, j)

    def column(other):
        return (other * 2 + core, s)

    def peer_at(offset):
        dx, dy = offset
        return (head // SIDE + dx) % SIDE * SIDE + (head % SIDE + dy) % SIDE

    def plane(h):
        return (g, h * 2 + half)

    loads = {
        name: pltpu.make_async_copy(src, dst, load_sem.at[i])
        for i, (name, src, dst) in enumerate(
            [
                ("in_weight", win_hbm, win),
                ("table", mod_hbm, mod),
                ("in_bias", bias_hbm, bias_ref),
                ("base", base_hbm, base),
                ("factors", fac_hbm, fac_ref),
                ("latent", latent_hbm.at[0], latent0),
                ("noise0", noise_hbm.at[0, 0], noise0),
                ("out_weight", wout_hbm, wout_half),
                ("order", order_hbm, order_ref),
                ("noise1", noise_hbm.at[0, 1], noise1),
            ]
        )
    }
    for load in loads.values():
        load.start()

    barrier = pltpu.get_barrier_semaphore()

    def greet(device):
        pl.semaphore_signal(barrier, inc=1, device_id=device, device_id_type=MESH)

    @pl.when(half == 0)
    def _():
        greet(partner)

    for j in range(zcount):
        other = column_target(j)

        @pl.when(other != zlo)
        def _():
            greet(column(other))

    for offset in OFFSETS:
        greet(plane(peer_at(offset)))
    greet(sibling)

    arriving, leaving = {}, {}

    start = start_ref[0]
    for name in ("in_weight", "in_bias", "table"):
        loads[name].wait()
    in_weight = win[...].astype(F32)
    in_bias = bias_ref[...]
    weight_centred = in_weight - jnp.mean(in_weight, axis=-1, keepdims=True)
    bias_centred = in_bias - jnp.mean(in_bias, axis=-1, keepdims=True)
    extra_row = lax.broadcasted_iota(jnp.int32, (16, D), 0)
    for step in range(STEPS):
        shift = mod[pl.ds(start + step, 1), :D]
        gain = 1.0 + mod[pl.ds(start + step, 1), D:]
        folded[step, :64, :] = (weight_centred * gain).astype(BF16)
        is_bias = (extra_row == 0) | (extra_row == 2)
        extra = jnp.where(is_bias, bias_centred * gain, jnp.where(extra_row == 1, shift, 0.0))
        folded[step, 64:80, :] = extra.astype(BF16)
        folded[step, 80:, :] = jnp.zeros((48, D), BF16)

    loads["base"].wait()
    half_lanes = pl.ds(pl.multiple_of(half * half_d, 128), half_d)
    for member in range(3):
        part = dot(folded[:, :, half_lanes].reshape(STEPS * 128, half_d), base[member, 0])
        for step in range(STEPS):
            piece = part[step * 128:(step + 1) * 128]
            own_part[step, :, member * HD:(member + 1) * HD] = piece
            part_out[step, :, member * HD:(member + 1) * HD] = piece[:ROWS].astype(BF16)

    loads["factors"].wait()
    store[core, zlo] = jnp.zeros(store.shape[2:], BF16)
    lanes = pl.ds(pl.multiple_of(head * 256, 256), 256)
    store[core, zlo, :store_rows, :] = fac_ref[:, lanes]
    for name in ("latent", "noise0", "out_weight"):
        loads[name].wait()
    own_rows = pl.ds(pl.multiple_of(half * own, own), own)
    other_rows = pl.ds(pl.multiple_of((1 - half) * own, own), own)
    pair_state[own_rows, :] = jnp.concatenate([latent0[...], noise0[...]], axis=1)
    packed = wout_half[...].astype(F32)
    wout[half] = jnp.concatenate([packed[:32], packed[32:]], axis=1).astype(BF16)
    for step in range(STEPS):
        maps_in[step, :, MAP_ROWS:, :] = jnp.zeros((heads, 128 - MAP_ROWS, 128), BF16)

    pl.semaphore_wait(barrier, zcount - 1 + 1 + heads - 1 + half)

    def arrived(name):
        arriving.pop(name)()

    def left(name):
        leaving.pop(name)()

    def column_copy(slot, other):
        place = store.at[core, slot]
        return pltpu.make_async_remote_copy(
            src_ref=place, dst_ref=place,
            send_sem=col_send.at[other], recv_sem=col_recv.at[slot],
            device_id=column(other), device_id_type=MESH,
        )

    def each_column(action):
        for j in range(zcount):
            other = column_target(j)

            @pl.when(other != zlo)
            def _():
                action(other)

    def pair_copy(i, src, dst, device=partner):
        return pltpu.make_async_remote_copy(
            src_ref=src, dst_ref=dst,
            send_sem=pair_send.at[i], recv_sem=pair_recv.at[i],
            device_id=device, device_id_type=MESH,
        )

    def exchange(name, i, out, into, device=partner):
        copy = pair_copy(i, out, out, device)
        copy.start()
        arriving[name] = pair_copy(i, into, into, device).wait_recv
        leaving[name] = copy.wait_send

    each_column(lambda other: column_copy(zlo, other).start())
    arriving["column"] = lambda: each_column(lambda other: column_copy(other, other).wait_recv())
    leaving["column"] = lambda: each_column(lambda other: column_copy(zlo, other).wait_send())
    state_copy = pair_copy(0, pair_state.at[own_rows], pair_state.at[own_rows])
    wout_copy = pair_copy(1, wout.at[half], wout.at[half])
    part_copies = [pair_copy(3 + step, part_out.at[step], part_in.at[step]) for step in range(STEPS)]

    def start_pair():
        state_copy.start()
        part_copies[0].start()
        wout_copy.start()

    @pl.when(half == 1)
    def _():
        pl.semaphore_signal(ready, inc=1, device_id=partner, device_id_type=MESH)
        start_pair()


    def plane_copy(kind, src, dst, peer, slot):
        return pltpu.make_async_remote_copy(
            src_ref=src, dst_ref=dst,
            send_sem=plane_send.at[kind, peer], recv_sem=plane_recv.at[kind, slot],
            device_id=plane(peer), device_id_type=MESH,
        )

    def send_plane(kind, src_of, place_of):
        def receive(offsets=OFFSETS):
            for offset in offsets:
                peer = peer_at(offset)
                plane_copy(kind, src_of(peer), place_of(peer), peer, peer).wait_recv()

        def finish():
            for offset in OFFSETS:
                peer = peer_at(offset)
                plane_copy(kind, src_of(peer), place_of(head), peer, head).wait_send()

        for offset in OFFSETS:
            peer = peer_at(offset)
            plane_copy(kind, src_of(peer), place_of(head), peer, head).start()
        arriving["plane", kind] = receive
        leaving["plane", kind] = finish
        return receive

    stored = zcount * 2 * store_rows
    row = lax.broadcasted_iota(jnp.int32, (stored, 256), 0)
    col = lax.broadcasted_iota(jnp.int32, (stored, 256), 1)
    in_block = col % block_rows
    slot = col // block_rows
    shard = slot % zcount * 2 + slot // zcount
    source = jnp.where(in_block < store_rows, shard * store_rows + in_block, -1)
    place = (row == source).astype(F32).astype(BF16)
    loads["order"].wait()
    order = jnp.broadcast_to((order_ref[...] + 1).astype(F32), (16, stored)).astype(BF16)
    order = dot(order, place)[0:1].astype(jnp.int32) - 1
    total = (pairs + heads) * 16
    line = lax.broadcasted_iota(jnp.int32, (total, 256), 0)
    entry = line & 15
    member_of = entry - 3 * ((entry * 11) >> 5)
    target = jnp.where(entry < 12, member_of * per_member + 2 * (line >> 4), -8)
    perm_even[...] = (target == order).astype(F32).astype(BF16)
    perm_odd[...] = (target + 1 == order).astype(F32).astype(BF16)

    arrived("column")
    exchange("sibling", 2, store.at[core], store.at[1 - core], sibling)
    arrived("sibling")
    blocks = store[...].reshape(256, 256)
    even = dot(perm_even[...], blocks)
    odd = dot(perm_odd[...], blocks)
    lane = lax.broadcasted_iota(jnp.int32, (total, 128), 1)
    entry = lax.broadcasted_iota(jnp.int32, (total, 128), 0) & 15
    rank = (entry * 11) >> 5
    even = jnp.where(rank < 2, even[:, :128], even[:, 128:])
    odd = jnp.where(rank < 2, odd[:, :128], odd[:, 128:])
    first = (rank & 1) == 0
    spread = jnp.where(
        lane < 64,
        jnp.where(first, even, pltpu.roll(even, 64, 1)),
        jnp.where(first, pltpu.roll(odd, 64, 1), odd),
    ).astype(BF16)
    lower = jnp.concatenate([spread[i * 16:(i + 1) * 16] for i in range(pairs)], axis=1)
    inner = [dot(lower, folded[step], NT).astype(BF16) for step in range(STEPS)]
    for other in range(heads):
        rank_out[other, :, 0:128] = inner[0]
        rank_out[other, :, 128:256] = inner[1]
        rank_out[other, :, 256:384] = spread[(pairs + other) * 16:(pairs + other + 1) * 16]
    rank_in[head] = rank_out[head]
    send_plane(0, lambda peer: rank_out.at[peer], lambda slot: rank_in.at[slot])

    @pl.when(half == 0)
    def _():
        pl.semaphore_wait(ready, 1)
        start_pair()

    part_copies[1].start()
    place = pair_state.at[other_rows]
    arriving["state"] = pair_copy(0, place, place).wait_recv
    place = wout.at[1 - half]
    arriving["out_weight"] = pair_copy(1, place, place).wait_recv
    leaving["state"] = state_copy.wait_send
    leaving["out_weight"] = wout_copy.wait_send
    for step in range(STEPS):
        arriving["part", step] = part_copies[step].wait_recv
        leaving["part", step] = part_copies[step].wait_send

    arrived("state")
    in_weight_bf = win[...]
    tokens[0, head] = token_features(pair_state[:, :C], in_weight_bf, in_bias)
    send_plane(1, lambda peer: tokens.at[0, head], lambda slot: tokens.at[0, slot])

    arrived(("plane", 0))
    ranks = rank_in[...].reshape(heads * 16, 384)
    entry = lax.broadcasted_iota(jnp.int32, (heads * 16, HD), 0) & 15
    member_of = entry - 3 * ((entry * 11) >> 5)
    upper = ranks[:, 256:].astype(F32)
    upper = jnp.concatenate(
        [jnp.where(member_of == member, upper, 0.0) for member in range(3)], axis=1
    ).astype(BF16)
    low_rank = dot(ranks[:, :256].astype(F32).T.astype(BF16), upper)
    arrived("out_weight")
    sides = [wout[i].astype(F32) for i in range(2)]
    out_weight = jnp.concatenate(
        [side[:, i * C:(i + 1) * C] for side in sides for i in range(2)], axis=0
    )
    got_maps = []

    def make_maps(step):
        arrived(("part", step))
        received = jnp.concatenate(
            [part_in[step].astype(F32), jnp.zeros((128 - ROWS, 3 * HD), F32)], axis=0
        )
        full = own_part[step] + received + low_rank[step * 128:(step + 1) * 128]
        to_score = HD ** (-0.5) * math.log2(math.e)
        queries, keys = full[:, :HD] * to_score, full[:, HD:2 * HD]
        score_map = exact_dot(queries[:ROWS], keys[:QUERY], NT)
        other_columns = exact_dot(keys[QUERY:ROWS], queries, NT)
        value_map = exact_dot(full[:ROWS, 2 * HD:], out_weight)
        maps_out[step, :ROWS, :] = jnp.concatenate([score_map, value_map], axis=1).astype(BF16)
        maps_out[step, ROWS:, :] = other_columns.astype(BF16)
        maps_in[step, head, :MAP_ROWS, :] = maps_out[step]

    def send_maps(step):
        got_maps.append(
            send_plane(
                2 + step,
                lambda peer: maps_out.at[step],
                lambda slot: maps_in.at[step, slot, pl.ds(0, MAP_ROWS)],
            )
        )

    make_maps(0)
    send_maps(0)
    make_maps(1)

    def first_lanes(features):
        lane = lax.broadcasted_iota(jnp.int32, features.shape, 1)
        return jnp.where(lane < KEY, features, jnp.zeros_like(features))

    def mapped(features, step, slots):
        features = first_lanes(features)
        lane = lax.broadcasted_iota(jnp.int32, features.shape, 1)
        result = []
        for slot in slots:
            maps = maps_in[step, slot]
            columns, others = dot(features, maps), dot(features, maps, NT)
            result.append(jnp.where(lane < QUERY, columns, jnp.where(lane < KEY, 0.0, others)))
        return jnp.concatenate(result, axis=0).astype(BF16)

    def attend(queries, keys, step, slots):
        count = queries.shape[0] // len(slots)
        exponent = jnp.exp2(dot(queries, keys, NT))
        weights = exponent * (1.0 / jnp.sum(exponent, axis=-1, keepdims=True))
        attended = first_lanes(dot(weights.astype(BF16), keys)).astype(BF16)
        sides = jnp.concatenate(
            [attended[i * count:(i + 1) * count] for i in range(len(slots))], axis=1
        )
        return dot(sides, jnp.concatenate([maps_in[step, slot] for slot in slots], axis=0))

    near_first = ((0, 0),) + OFFSETS[::-1]

    arrived(("plane", 1))
    keys = tokens[0].reshape(heads * both, 128)
    features = tokens[0, head]
    arriving.pop(("plane", 2))
    velocity = jnp.zeros((both, 128), F32)
    for i in range(0, heads, 4):
        offsets = near_first[i:i + 4]
        got_maps[0](offsets[1:] if i == 0 else offsets)
        slots = [peer_at(offset) for offset in offsets]
        if i + 4 == heads:
            send_maps(1)
        velocity += attend(mapped(features, 0, slots), keys, 0, slots)
    left("state")
    pair_state[:, :C] = advance(pair_state[:, :C], velocity[:, C:], pair_state[:, C:], start)
    tokens[1, head] = token_features(pair_state[:, :C], in_weight_bf, in_bias)
    send_plane(4, lambda peer: tokens.at[1, head], lambda slot: tokens.at[1, slot])
    arrived(("plane", 3))
    slots = [peer_at(offset) for offset in near_first]
    queries = mapped(tokens[1, head, own_rows, :], 1, slots)
    arrived(("plane", 4))

    keys = tokens[1].reshape(heads * both, 128)
    velocity = jnp.zeros((own, 128), F32)
    for i in range(0, heads, 8):
        velocity += attend(queries[i * own:(i + 8) * own], keys, 1, slots[i:i + 8])
    velocity = velocity[:, C:]
    loads["noise1"].wait()
    latent_out[0] = advance(pair_state[own_rows, :C], velocity, noise1[...], start + 1)
    velocity_out[0] = velocity

    for name in list(leaving):
        left(name)


def shards(groups, heads):
    def run(
        latent, step_noise, start_index, mod_table, in_weight, in_bias,
        base_weight, factor_store, block_order, out_weight,
    ):
        own = latent.shape[1]
        block_rows = (factor_store.shape[0] + 15) // 16 * 16
        total = (D // 128 + heads) * 16
        vmem = pl.BlockSpec(memory_space=pltpu.VMEM)
        anywhere = pl.BlockSpec(memory_space=pl.ANY)
        return pl.pallas_call(
            functools.partial(kernel, groups, heads),
            out_shape=(
                jax.ShapeDtypeStruct(latent.shape, F32),
                jax.ShapeDtypeStruct(latent.shape, F32),
            ),
            in_specs=[
                pl.BlockSpec(memory_space=pltpu.SMEM),
                *[anywhere] * 9,
            ],
            out_specs=(vmem, vmem),
            scratch_shapes=[
                pltpu.VMEM(mod_table.shape, F32),
                pltpu.VMEM(in_weight.shape, BF16),
                pltpu.VMEM((1, D), F32),
                pltpu.VMEM(base_weight.shape, BF16),
                pltpu.VMEM(factor_store.shape, BF16),
                pltpu.VMEM((1, block_order.shape[0]), jnp.int32),
                pltpu.VMEM((own, C), F32),
                pltpu.VMEM((own, C), F32),
                pltpu.VMEM((own, C), F32),
                pltpu.VMEM(out_weight.shape, BF16),
                pltpu.VMEM((2 * own, 128), F32),
                pltpu.VMEM((2, 32, 128), BF16),
                pltpu.VMEM((2, groups // 2, block_rows, 256), BF16),
                pltpu.VMEM((total, 256), BF16),
                pltpu.VMEM((total, 256), BF16),
                pltpu.VMEM((STEPS, 128, D), BF16),
                pltpu.VMEM((STEPS, 128, 3 * HD), F32),
                pltpu.VMEM((STEPS, ROWS, 3 * HD), BF16),
                pltpu.VMEM((STEPS, ROWS, 3 * HD), BF16),
                pltpu.VMEM((heads, 16, 384), BF16),
                pltpu.VMEM((heads, 16, 384), BF16),
                pltpu.VMEM((STEPS, heads, 2 * own, 128), BF16),
                pltpu.VMEM((STEPS, MAP_ROWS, 128), BF16),
                pltpu.VMEM((STEPS, heads, 128, 128), BF16),
                pltpu.SemaphoreType.DMA((10,)),
                pltpu.SemaphoreType.DMA((groups // 2,)),
                pltpu.SemaphoreType.DMA((groups // 2,)),
                pltpu.SemaphoreType.DMA((5,)),
                pltpu.SemaphoreType.DMA((5,)),
                pltpu.SemaphoreType.DMA((5, heads)),
                pltpu.SemaphoreType.DMA((5, heads)),
                pltpu.SemaphoreType.REGULAR,
            ],
            compiler_params=pltpu.CompilerParams(
                collective_id=0, has_side_effects=True, vmem_limit_bytes=63 * 1024 * 1024
            ),
        )(
            start_index, latent, step_noise, mod_table, in_weight, in_bias.reshape(1, -1),
            base_weight, factor_store, block_order.reshape(1, -1), out_weight,
        )

    return run


def solution(mesh):
    in_specs = (
        P("grp", "seq", None),
        P("grp", None, "seq", None),
        P("grp"),
        P(),
        P(),
        P(),
        P(None, "seq", None, None),
        P("grp", None),
        P(),
        P("seq", None),
    )
    out_specs = (P("grp", "seq", None), P("grp", "seq", None))
    run = shards(mesh.shape["grp"], mesh.shape["seq"] // 2)
    return jax.shard_map(run, mesh=mesh, in_specs=in_specs, out_specs=out_specs, check_vma=False)
```

time: 78 us -> 59.8 us (0.77)
  the two profiles are of different devices: /device:TPU:64 before, /device:TPU:1 now
where the time goes in v2:
time: 59.8 us; the launch traced here: 59.5 us
  Pallas kernels  55.6 us (93%)
  local copies, waits for them, and re-layouts  2.65 us (4%)
  between operations  1.29 us (2%)
    pallas_call x1, Pallas kernels, run(): pl.pallas_call(functools.partial(kernel, groups, heads), out_shape=(jax.S...  55.6 us
    unnamed x2, local copies, waits for them, and re-layouts  2.65 us

profile of v2, /device:TPU:1, one launch (start us, length us, event | category | flops | bytes accessed | tf_op | source)
XLA Modules:
  0.0 59.5 jit_solution(16905555961331401988)
XLA Ops:
  1.3 55.6 %shard_map.113 = (f32[1,32,64]{2,1,0:T(8,128)}, f32[1,32,64]{2,1,0:T(8,128)}) custom-call(s32[1]{0:T(128)S(6)} %copy.14.start_ref, f32[1,32,64]{2,1,0:T(8,128)} %latent_hbm.1, f32[1,2,32,64]{3,2,1,0:T(8,128)} %noise_hbm.1, f32[10,6144]{1,0:T(8,128)} %mod_hbm.1, bf16[64,3072]{1,0:T(8,128)(2,1)} %win_hbm.1, f32[1,3072]{1,0:T(1,128)} %bitcast.2, ...), custom_call_target="tpu_custom_call" | custom-call | tf_op jit(solution)/shard_map/pallas_call | solution.py:461
  56.8 1.3 %copy.15 = f32[1,32,64]{2,1,0:T(8,128)} copy(f32[1,32,64]{2,1,0:T(8,128)} %get-tuple-element.4) | data formatting | bytes 16384
  58.2 1.3 %copy.16 = f32[1,32,64]{2,1,0:T(8,128)} copy(f32[1,32,64]{2,1,0:T(8,128)} %get-tuple-element.5) | data formatting | bytes 16384

commit v3 on v2

--- a/solution.py
+++ b/solution.py
@@ -81,7 +81,7 @@
 def kernel(
     groups, heads,
     start_ref, latent_hbm, noise_hbm, mod_hbm, win_hbm, bias_hbm, base_hbm, fac_hbm, order_hbm, wout_hbm,
-    latent_out, velocity_out,
+    result,
     mod, win, bias_ref, base, fac_ref, order_ref, latent0, noise0, noise1, wout_half,
     pair_state, wout, store, perm_even, perm_odd, folded,
     own_part, part_out, part_in, rank_out, rank_in, tokens, maps_out, maps_in,
@@ -133,9 +133,6 @@
             ]
         )
     }
-    for load in loads.values():
-        load.start()
-
     barrier = pltpu.get_barrier_semaphore()
 
     def greet(device):
@@ -155,6 +152,8 @@
     for offset in OFFSETS:
         greet(plane(peer_at(offset)))
     greet(sibling)
+    for load in loads.values():
+        load.start()
 
     arriving, leaving = {}, {}
 
@@ -177,12 +176,17 @@
 
     loads["base"].wait()
     half_lanes = pl.ds(pl.multiple_of(half * half_d, 128), half_d)
+    extras = [[None] * 3 for _ in range(STEPS)]
     for member in range(3):
         part = dot(folded[:, :, half_lanes].reshape(STEPS * 128, half_d), base[member, 0])
         for step in range(STEPS):
             piece = part[step * 128:(step + 1) * 128]
             own_part[step, :, member * HD:(member + 1) * HD] = piece
-            part_out[step, :, member * HD:(member + 1) * HD] = piece[:ROWS].astype(BF16)
+            part_out[step, member * QUERY:(member + 1) * QUERY, :] = piece[:QUERY].astype(BF16)
+            extras[step][member] = piece[QUERY:QUERY + 2]
+    for step in range(STEPS):
+        rest = jnp.concatenate(extras[step] + [jnp.zeros((10, HD), F32)], axis=0)
+        part_out[step, 3 * QUERY:, :] = rest.astype(BF16)
 
     loads["factors"].wait()
     store[core, zlo] = jnp.zeros(store.shape[2:], BF16)
@@ -243,9 +247,9 @@
     part_copies = [pair_copy(3 + step, part_out.at[step], part_in.at[step]) for step in range(STEPS)]
 
     def start_pair():
-        state_copy.start()
         part_copies[0].start()
         wout_copy.start()
+        state_copy.start()
 
     @pl.when(half == 1)
     def _():
@@ -362,8 +366,22 @@
 
     def make_maps(step):
         arrived(("part", step))
+        received = part_in[step].astype(F32)
+        rest = received[3 * QUERY:]
         received = jnp.concatenate(
-            [part_in[step].astype(F32), jnp.zeros((128 - ROWS, 3 * HD), F32)], axis=0
+            [
+                jnp.concatenate(
+                    [
+                        received[member * QUERY:(member + 1) * QUERY],
+                        rest[2 * member:2 * member + 2],
+                        rest[2 * member:2 * member + 1],
+                        jnp.zeros((128 - QUERY - 3, HD), F32),
+                    ],
+                    axis=0,
+                )
+                for member in range(3)
+            ],
+            axis=1,
         )
         full = own_part[step] + received + low_rank[step * 128:(step + 1) * 128]
         to_score = HD ** (-0.5) * math.log2(math.e)
@@ -423,7 +441,7 @@
         offsets = near_first[i:i + 4]
         got_maps[0](offsets[1:] if i == 0 else offsets)
         slots = [peer_at(offset) for offset in offsets]
-        if i + 4 == heads:
+        if i == 4:
             send_maps(1)
         velocity += attend(mapped(features, 0, slots), keys, 0, slots)
     left("state")
@@ -441,8 +459,8 @@
         velocity += attend(queries[i * own:(i + 8) * own], keys, 1, slots[i:i + 8])
     velocity = velocity[:, C:]
     loads["noise1"].wait()
-    latent_out[0] = advance(pair_state[own_rows, :C], velocity, noise1[...], start + 1)
-    velocity_out[0] = velocity
+    latent = advance(pair_state[own_rows, :C], velocity, noise1[...], start + 1)
+    result[0] = jnp.concatenate([latent, velocity], axis=1)
 
     for name in list(leaving):
         left(name)
@@ -458,17 +476,14 @@
         total = (D // 128 + heads) * 16
         vmem = pl.BlockSpec(memory_space=pltpu.VMEM)
         anywhere = pl.BlockSpec(memory_space=pl.ANY)
-        return pl.pallas_call(
+        result = pl.pallas_call(
             functools.partial(kernel, groups, heads),
-            out_shape=(
-                jax.ShapeDtypeStruct(latent.shape, F32),
-                jax.ShapeDtypeStruct(latent.shape, F32),
-            ),
+            out_shape=jax.ShapeDtypeStruct((1, own, 2 * C), F32),
             in_specs=[
                 pl.BlockSpec(memory_space=pltpu.SMEM),
                 *[anywhere] * 9,
             ],
-            out_specs=(vmem, vmem),
+            out_specs=vmem,
             scratch_shapes=[
                 pltpu.VMEM(mod_table.shape, F32),
                 pltpu.VMEM(in_weight.shape, BF16),
@@ -487,8 +502,8 @@
                 pltpu.VMEM((total, 256), BF16),
                 pltpu.VMEM((STEPS, 128, D), BF16),
                 pltpu.VMEM((STEPS, 128, 3 * HD), F32),
-                pltpu.VMEM((STEPS, ROWS, 3 * HD), BF16),
-                pltpu.VMEM((STEPS, ROWS, 3 * HD), BF16),
+                pltpu.VMEM((STEPS, 3 * QUERY + 16, HD), BF16),
+                pltpu.VMEM((STEPS, 3 * QUERY + 16, HD), BF16),
                 pltpu.VMEM((heads, 16, 384), BF16),
                 pltpu.VMEM((heads, 16, 384), BF16),
                 pltpu.VMEM((STEPS, heads, 2 * own, 128), BF16),
@@ -510,6 +525,7 @@
             start_index, latent, step_noise, mod_table, in_weight, in_bias.reshape(1, -1),
             base_weight, factor_store, block_order.reshape(1, -1), out_weight,
         )
+        return result[:, :, :C], result[:, :, C:]
 
     return run
 

time: 59.8 us -> 54.7 us (0.915)
  the two profiles are of different devices: /device:TPU:1 before, /device:TPU:290 now
where the time goes in v3:
time: 54.7 us; the launch traced here: 54.5 us
  Pallas kernels  51.7 us (95%)
  local copies, waits for them, and re-layouts  1.47 us (3%)
  between operations  1.29 us (2%)
    pallas_call x1, Pallas kernels, run(): pl.pallas_call(functools.partial(kernel, groups, heads), out_shape=jax.Sh...  51.7 us
    slice x1, local copies, waits for them, and re-layouts, run(): return (result[:, :, :C], result[:, :, C:])  1.47 us

profile of v3, /device:TPU:290, one launch (start us, length us, event | category | flops | bytes accessed | tf_op | source)
XLA Modules:
  0.0 54.5 jit_solution(18078820710695836748)
XLA Ops:
  1.3 51.7 %shard_map.113 = f32[1,32,128]{2,1,0:T(8,128)} custom-call(s32[1]{0:T(128)S(6)} %copy.12.start_ref, f32[1,32,64]{2,1,0:T(8,128)} %latent_hbm.1, f32[1,2,32,64]{3,2,1,0:T(8,128)} %noise_hbm.1, f32[10,6144]{1,0:T(8,128)} %mod_hbm.1, bf16[64,3072]{1,0:T(8,128)(2,1)} %win_hbm.1, f32[1,3072]{1,0:T(1,128)} %bitcast.2, bf16[3,1,1536,128]{3,2,1,0:T(8,128)(2,1)} %base_hbm.1, ...), custom_call_target="tpu_custom_call" | custom-call | tf_op jit(solution)/shard_map/pallas_call | solution.py:479
  53.0 1.5 %fusion = (f32[1,32,64]{2,1,0:T(8,128)}, f32[1,32,64]{2,1,0:T(8,128)}) fusion(f32[1,32,128]{2,1,0:T(8,128)} %shard_map.113), kind=kLoop, calls=%fused_computation | loop fusion | bytes 32768 | tf_op jit(solution)/shard_map/slice | solution.py:528

commit v4 on v3

--- a/solution.py
+++ b/solution.py
@@ -52,17 +52,29 @@
     return (sigma_now, sigma_step, spread)
 
 
-def advance(state, velocity, noise, index):
+def carried(state, noise, index):
     sigma_now, sigma_step, spread = plan(jnp.full(state.shape, index, jnp.int32))
     return (
         state * (1.0 + spread * spread / (2.0 * sigma_now) * sigma_step)
-        + velocity * (1.0 + spread * spread * (1.0 - sigma_now) / (2.0 * sigma_now)) * sigma_step
         + spread * jnp.sqrt(-sigma_step) * noise
     )
 
 
-def token_features(state, in_weight, in_bias):
-    latent_in = state.astype(BF16)
+def added(velocity, index):
+    sigma_now, sigma_step, spread = plan(jnp.full(velocity.shape, index, jnp.int32))
+    return velocity * (1.0 + spread * spread * (1.0 - sigma_now) / (2.0 * sigma_now)) * sigma_step
+
+
+def pack(rows):
+    count = rows.shape[0] // 2
+    return jnp.concatenate([rows[:count], rows[count:]], axis=1)
+
+
+def unpack(rows):
+    return jnp.concatenate([rows[:, :64], rows[:, 64:]], axis=0)
+
+
+def token_features(latent_in, in_weight, in_bias):
     hidden = dot(latent_in, in_weight) + in_bias
     average = jnp.mean(hidden, axis=-1, keepdims=True)
     centred = hidden - average
@@ -83,9 +95,9 @@
     start_ref, latent_hbm, noise_hbm, mod_hbm, win_hbm, bias_hbm, base_hbm, fac_hbm, order_hbm, wout_hbm,
     result,
     mod, win, bias_ref, base, fac_ref, order_ref, latent0, noise0, noise1, wout_half,
-    pair_state, wout, store, perm_even, perm_odd, folded,
+    hello, carry, state, store, perm_even, perm_odd, folded,
     own_part, part_out, part_in, rank_out, rank_in, tokens, maps_out, maps_in,
-    load_sem, col_send, col_recv, pair_send, pair_recv, plane_send, plane_recv, ready,
+    load_sem, col_send, col_recv, pair_send, pair_recv, plane_send, plane_recv, ready, heard,
 ):
     g = lax.axis_index("grp")
     s = lax.axis_index("seq")
@@ -120,11 +132,11 @@
         name: pltpu.make_async_copy(src, dst, load_sem.at[i])
         for i, (name, src, dst) in enumerate(
             [
+                ("factors", fac_hbm, fac_ref),
                 ("in_weight", win_hbm, win),
                 ("table", mod_hbm, mod),
                 ("in_bias", bias_hbm, bias_ref),
                 ("base", base_hbm, base),
-                ("factors", fac_hbm, fac_ref),
                 ("latent", latent_hbm.at[0], latent0),
                 ("noise0", noise_hbm.at[0, 0], noise0),
                 ("out_weight", wout_hbm, wout_half),
@@ -140,22 +152,62 @@
 
     @pl.when(half == 0)
     def _():
-        greet(partner)
+        greet((zlo * 2, s + 1))
 
     for j in range(zcount):
         other = column_target(j)
 
         @pl.when(other != zlo)
         def _():
-            greet(column(other))
+            greet((other * 2 + half, s))
 
     for offset in OFFSETS:
-        greet(plane(peer_at(offset)))
+        greet((zlo * 2 + 1, peer_at(offset) * 2 + half))
     greet(sibling)
+    in_columns, in_planes = 2 * (zcount - 1), 2 * (heads - 1)
+
     for load in loads.values():
         load.start()
 
     arriving, leaving = {}, {}
+
+    def column_copy(slot, other):
+        place = store.at[core, slot]
+        return pltpu.make_async_remote_copy(
+            src_ref=place, dst_ref=place,
+            send_sem=col_send.at[other], recv_sem=col_recv.at[slot],
+            device_id=column(other), device_id_type=MESH,
+        )
+
+    def each_column(action):
+        for j in range(zcount):
+            other = column_target(j)
+
+            @pl.when(other != zlo)
+            def _():
+                action(other)
+
+    @pl.when(core == 0)
+    def _():
+        pl.semaphore_wait(barrier, 1 + jnp.where(half == 0, in_columns, 2))
+        pl.semaphore_signal(heard, inc=1, device_id=sibling, device_id_type=MESH)
+
+    @pl.when(core == 1)
+    def _():
+        pl.semaphore_wait(heard, 1)
+
+    @pl.when(half == 1)
+    def _():
+        pl.semaphore_signal(ready, inc=1, device_id=partner, device_id_type=MESH)
+
+    loads["factors"].wait()
+    store[core, zlo] = jnp.zeros(store.shape[2:], BF16)
+    lanes = pl.ds(pl.multiple_of(head * 256, 256), 256)
+    store[core, zlo, :store_rows, :] = fac_ref[:, lanes]
+
+    @pl.when(half == 0)
+    def _():
+        each_column(lambda other: column_copy(zlo, other).start())
 
     start = start_ref[0]
     for name in ("in_weight", "in_bias", "table"):
@@ -188,43 +240,20 @@
         rest = jnp.concatenate(extras[step] + [jnp.zeros((10, HD), F32)], axis=0)
         part_out[step, 3 * QUERY:, :] = rest.astype(BF16)
 
-    loads["factors"].wait()
-    store[core, zlo] = jnp.zeros(store.shape[2:], BF16)
-    lanes = pl.ds(pl.multiple_of(head * 256, 256), 256)
-    store[core, zlo, :store_rows, :] = fac_ref[:, lanes]
     for name in ("latent", "noise0", "out_weight"):
         loads[name].wait()
+    hello[half, :own // 2, :] = pack(latent0[...]).astype(BF16)
+    hello[half, own // 2:, :] = pack(wout_half[...].astype(F32)).astype(BF16)
+    carry[half] = pack(carried(latent0[...], noise0[...], start))
     own_rows = pl.ds(pl.multiple_of(half * own, own), own)
-    other_rows = pl.ds(pl.multiple_of((1 - half) * own, own), own)
-    pair_state[own_rows, :] = jnp.concatenate([latent0[...], noise0[...]], axis=1)
-    packed = wout_half[...].astype(F32)
-    wout[half] = jnp.concatenate([packed[:32], packed[32:]], axis=1).astype(BF16)
     for step in range(STEPS):
         maps_in[step, :, MAP_ROWS:, :] = jnp.zeros((heads, 128 - MAP_ROWS, 128), BF16)
 
-    pl.semaphore_wait(barrier, zcount - 1 + 1 + heads - 1 + half)
-
     def arrived(name):
         arriving.pop(name)()
 
     def left(name):
         leaving.pop(name)()
-
-    def column_copy(slot, other):
-        place = store.at[core, slot]
-        return pltpu.make_async_remote_copy(
-            src_ref=place, dst_ref=place,
-            send_sem=col_send.at[other], recv_sem=col_recv.at[slot],
-            device_id=column(other), device_id_type=MESH,
-        )
-
-    def each_column(action):
-        for j in range(zcount):
-            other = column_target(j)
-
-            @pl.when(other != zlo)
-            def _():
-                action(other)
 
     def pair_copy(i, src, dst, device=partner):
         return pltpu.make_async_remote_copy(
@@ -239,23 +268,30 @@
         arriving[name] = pair_copy(i, into, into, device).wait_recv
         leaving[name] = copy.wait_send
 
-    each_column(lambda other: column_copy(zlo, other).start())
+    hello_copy = pair_copy(0, hello.at[half], hello.at[half])
+    carry_copy = pair_copy(1, carry.at[half], carry.at[half])
+    part_copies = [pair_copy(3 + step, part_out.at[step], part_in.at[step]) for step in range(STEPS)]
+
+    def start_pair():
+        hello_copy.start()
+        part_copies[0].start()
+
+    @pl.when(core == 1)
+    def _():
+        pl.semaphore_wait(barrier, 1 + in_planes + jnp.where(half == 0, 0, in_columns))
+        pl.semaphore_signal(heard, inc=1, device_id=sibling, device_id_type=MESH)
+
+    @pl.when(core == 0)
+    def _():
+        pl.semaphore_wait(heard, 1)
+
+    @pl.when(half == 1)
+    def _():
+        each_column(lambda other: column_copy(zlo, other).start())
+        start_pair()
+
     arriving["column"] = lambda: each_column(lambda other: column_copy(other, other).wait_recv())
     leaving["column"] = lambda: each_column(lambda other: column_copy(zlo, other).wait_send())
-    state_copy = pair_copy(0, pair_state.at[own_rows], pair_state.at[own_rows])
-    wout_copy = pair_copy(1, wout.at[half], wout.at[half])
-    part_copies = [pair_copy(3 + step, part_out.at[step], part_in.at[step]) for step in range(STEPS)]
-
-    def start_pair():
-        part_copies[0].start()
-        wout_copy.start()
-        state_copy.start()
-
-    @pl.when(half == 1)
-    def _():
-        pl.semaphore_signal(ready, inc=1, device_id=partner, device_id_type=MESH)
-        start_pair()
-
 
     def plane_copy(kind, src, dst, peer, slot):
         return pltpu.make_async_remote_copy(
@@ -303,6 +339,12 @@
 
     arrived("column")
     exchange("sibling", 2, store.at[core], store.at[1 - core], sibling)
+
+    @pl.when(half == 0)
+    def _():
+        pl.semaphore_wait(ready, 1)
+        start_pair()
+
     arrived("sibling")
     blocks = store[...].reshape(256, 256)
     even = dot(perm_even[...], blocks)
@@ -327,25 +369,21 @@
     rank_in[head] = rank_out[head]
     send_plane(0, lambda peer: rank_out.at[peer], lambda slot: rank_in.at[slot])
 
-    @pl.when(half == 0)
-    def _():
-        pl.semaphore_wait(ready, 1)
-        start_pair()
-
+    carry_copy.start()
     part_copies[1].start()
-    place = pair_state.at[other_rows]
-    arriving["state"] = pair_copy(0, place, place).wait_recv
-    place = wout.at[1 - half]
-    arriving["out_weight"] = pair_copy(1, place, place).wait_recv
-    leaving["state"] = state_copy.wait_send
-    leaving["out_weight"] = wout_copy.wait_send
+    for name, i, buffer, copy in (("hello", 0, hello, hello_copy), ("carry", 1, carry, carry_copy)):
+        arriving[name] = pair_copy(i, buffer.at[1 - half], buffer.at[1 - half]).wait_recv
+        leaving[name] = copy.wait_send
     for step in range(STEPS):
         arriving["part", step] = part_copies[step].wait_recv
         leaving["part", step] = part_copies[step].wait_send
 
-    arrived("state")
+    arrived("hello")
     in_weight_bf = win[...]
-    tokens[0, head] = token_features(pair_state[:, :C], in_weight_bf, in_bias)
+    latent_in = jnp.concatenate(
+        [unpack(hello[i, :own // 2, :].astype(F32)) for i in range(2)], axis=0
+    ).astype(BF16)
+    tokens[0, head] = token_features(latent_in, in_weight_bf, in_bias)
     send_plane(1, lambda peer: tokens.at[0, head], lambda slot: tokens.at[0, slot])
 
     arrived(("plane", 0))
@@ -357,10 +395,8 @@
         [jnp.where(member_of == member, upper, 0.0) for member in range(3)], axis=1
     ).astype(BF16)
     low_rank = dot(ranks[:, :256].astype(F32).T.astype(BF16), upper)
-    arrived("out_weight")
-    sides = [wout[i].astype(F32) for i in range(2)]
     out_weight = jnp.concatenate(
-        [side[:, i * C:(i + 1) * C] for side in sides for i in range(2)], axis=0
+        [unpack(hello[i, own // 2:, :].astype(F32)) for i in range(2)], axis=0
     )
     got_maps = []
 
@@ -444,9 +480,10 @@
         if i == 4:
             send_maps(1)
         velocity += attend(mapped(features, 0, slots), keys, 0, slots)
-    left("state")
-    pair_state[:, :C] = advance(pair_state[:, :C], velocity[:, C:], pair_state[:, C:], start)
-    tokens[1, head] = token_features(pair_state[:, :C], in_weight_bf, in_bias)
+    arrived("carry")
+    carry_rows = jnp.concatenate([unpack(carry[i]) for i in range(2)], axis=0)
+    state[...] = carry_rows + added(velocity[:, C:], start)
+    tokens[1, head] = token_features(state[...].astype(BF16), in_weight_bf, in_bias)
     send_plane(4, lambda peer: tokens.at[1, head], lambda slot: tokens.at[1, slot])
     arrived(("plane", 3))
     slots = [peer_at(offset) for offset in near_first]
@@ -459,7 +496,7 @@
         velocity += attend(queries[i * own:(i + 8) * own], keys, 1, slots[i:i + 8])
     velocity = velocity[:, C:]
     loads["noise1"].wait()
-    latent = advance(pair_state[own_rows, :C], velocity, noise1[...], start + 1)
+    latent = carried(state[own_rows, :], noise1[...], start + 1) + added(velocity, start + 1)
     result[0] = jnp.concatenate([latent, velocity], axis=1)
 
     for name in list(leaving):
@@ -495,8 +532,9 @@
                 pltpu.VMEM((own, C), F32),
                 pltpu.VMEM((own, C), F32),
                 pltpu.VMEM(out_weight.shape, BF16),
-                pltpu.VMEM((2 * own, 128), F32),
-                pltpu.VMEM((2, 32, 128), BF16),
+                pltpu.VMEM((2, own // 2 + 32, 128), BF16),
+                pltpu.VMEM((2, own // 2, 128), F32),
+                pltpu.VMEM((2 * own, C), F32),
                 pltpu.VMEM((2, groups // 2, block_rows, 256), BF16),
                 pltpu.VMEM((total, 256), BF16),
                 pltpu.VMEM((total, 256), BF16),
@@ -517,6 +555,7 @@
                 pltpu.SemaphoreType.DMA((5, heads)),
                 pltpu.SemaphoreType.DMA((5, heads)),
                 pltpu.SemaphoreType.REGULAR,
+                pltpu.SemaphoreType.REGULAR,
             ],
             compiler_params=pltpu.CompilerParams(
                 collective_id=0, has_side_effects=True, vmem_limit_bytes=63 * 1024 * 1024

time: 54.7 us -> 51.5 us (0.941)
  the two profiles are of different devices: /device:TPU:290 before, /device:TPU:1 now
where the time goes in v4:
time: 51.5 us; the launch traced here: 51.3 us
  Pallas kernels  48.6 us (94%)
  local copies, waits for them, and re-layouts  1.47 us (3%)
  between operations  1.29 us (3%)
    pallas_call x1, Pallas kernels, run(): pl.pallas_call(functools.partial(kernel, groups, heads), out_shape=jax.Sh...  48.6 us
    slice x1, local copies, waits for them, and re-layouts, run(): return (result[:, :, :C], result[:, :, C:])  1.47 us

profile of v4, /device:TPU:1, one launch (start us, length us, event | category | flops | bytes accessed | tf_op | source)
XLA Modules:
  0.0 51.3 jit_solution(11422080412909857652)
XLA Ops:
  1.3 48.6 %shard_map.113 = f32[1,32,128]{2,1,0:T(8,128)} custom-call(s32[1]{0:T(128)S(6)} %copy.12.start_ref, f32[1,32,64]{2,1,0:T(8,128)} %latent_hbm.1, f32[1,2,32,64]{3,2,1,0:T(8,128)} %noise_hbm.1, f32[10,6144]{1,0:T(8,128)} %mod_hbm.1, bf16[64,3072]{1,0:T(8,128)(2,1)} %win_hbm.1, f32[1,3072]{1,0:T(1,128)} %bitcast.2, bf16[3,1,1536,128]{3,2,1,0:T(8,128)(2,1)} %base_hbm.1, ...), custom_call_target="tpu_custom_call" | custom-call | tf_op jit(solution)/shard_map/pallas_call | solution.py:516
  49.9 1.5 %fusion = (f32[1,32,64]{2,1,0:T(8,128)}, f32[1,32,64]{2,1,0:T(8,128)}) fusion(f32[1,32,128]{2,1,0:T(8,128)} %shard_map.113), kind=kLoop, calls=%fused_computation | loop fusion | bytes 32768 | tf_op jit(solution)/shard_map/slice | solution.py:567

commit v5 on v4

--- a/solution.py
+++ b/solution.py
@@ -145,6 +145,8 @@
             ]
         )
     }
+    loads["factors"].start()
+
     barrier = pltpu.get_barrier_semaphore()
 
     def greet(device):
@@ -166,8 +168,8 @@
     greet(sibling)
     in_columns, in_planes = 2 * (zcount - 1), 2 * (heads - 1)
 
-    for load in loads.values():
-        load.start()
+    for name in list(loads)[1:]:
+        loads[name].start()
 
     arriving, leaving = {}, {}
 
@@ -275,6 +277,10 @@
     def start_pair():
         hello_copy.start()
         part_copies[0].start()
+
+    def start_late_pair():
+        carry_copy.start()
+        part_copies[1].start()
 
     @pl.when(core == 1)
     def _():
@@ -344,6 +350,10 @@
     def _():
         pl.semaphore_wait(ready, 1)
         start_pair()
+
+    @pl.when(half == 1)
+    def _():
+        start_late_pair()
 
     arrived("sibling")
     blocks = store[...].reshape(256, 256)
@@ -369,8 +379,10 @@
     rank_in[head] = rank_out[head]
     send_plane(0, lambda peer: rank_out.at[peer], lambda slot: rank_in.at[slot])
 
-    carry_copy.start()
-    part_copies[1].start()
+    @pl.when(half == 0)
+    def _():
+        start_late_pair()
+
     for name, i, buffer, copy in (("hello", 0, hello, hello_copy), ("carry", 1, carry, carry_copy)):
         arriving[name] = pair_copy(i, buffer.at[1 - half], buffer.at[1 - half]).wait_recv
         leaving[name] = copy.wait_send
@@ -441,6 +453,7 @@
     make_maps(0)
     send_maps(0)
     make_maps(1)
+    send_maps(1)
 
     def first_lanes(features):
         lane = lax.broadcasted_iota(jnp.int32, features.shape, 1)
@@ -477,8 +490,6 @@
         offsets = near_first[i:i + 4]
         got_maps[0](offsets[1:] if i == 0 else offsets)
         slots = [peer_at(offset) for offset in offsets]
-        if i == 4:
-            send_maps(1)
         velocity += attend(mapped(features, 0, slots), keys, 0, slots)
     arrived("carry")
     carry_rows = jnp.concatenate([unpack(carry[i]) for i in range(2)], axis=0)

time: 51.5 us -> 50.8 us (0.986)
  the two profiles are of different devices: /device:TPU:1 before, /device:TPU:448 now
where the time goes in v5:
time: 50.8 us; the launch traced here: 50.6 us
  Pallas kernels  47.9 us (94%)
  local copies, waits for them, and re-layouts  1.47 us (3%)
  between operations  1.29 us (3%)
    pallas_call x1, Pallas kernels, run(): pl.pallas_call(functools.partial(kernel, groups, heads), out_shape=jax.Sh...  47.9 us
    slice x1, local copies, waits for them, and re-layouts, run(): return (result[:, :, :C], result[:, :, C:])  1.47 us

profile of v5, /device:TPU:448, one launch (start us, length us, event | category | flops | bytes accessed | tf_op | source)
XLA Modules:
  0.0 50.6 jit_solution(7638912014681083487)
XLA Ops:
  1.3 47.9 %shard_map.113 = f32[1,32,128]{2,1,0:T(8,128)} custom-call(s32[1]{0:T(128)S(6)} %copy.12.start_ref, f32[1,32,64]{2,1,0:T(8,128)} %latent_hbm.1, f32[1,2,32,64]{3,2,1,0:T(8,128)} %noise_hbm.1, f32[10,6144]{1,0:T(8,128)} %mod_hbm.1, bf16[64,3072]{1,0:T(8,128)(2,1)} %win_hbm.1, f32[1,3072]{1,0:T(1,128)} %bitcast.2, bf16[3,1,1536,128]{3,2,1,0:T(8,128)(2,1)} %base_hbm.1, ...), custom_call_target="tpu_custom_call" | custom-call | tf_op jit(solution)/shard_map/pallas_call | solution.py:527
  49.2 1.5 %fusion = (f32[1,32,64]{2,1,0:T(8,128)}, f32[1,32,64]{2,1,0:T(8,128)}) fusion(f32[1,32,128]{2,1,0:T(8,128)} %shard_map.113), kind=kLoop, calls=%fused_computation | loop fusion | bytes 32768 | tf_op jit(solution)/shard_map/slice | solution.py:578

commit v6 on v5

--- a/solution.py
+++ b/solution.py
@@ -275,12 +275,15 @@
     part_copies = [pair_copy(3 + step, part_out.at[step], part_in.at[step]) for step in range(STEPS)]
 
     def start_pair():
-        hello_copy.start()
         part_copies[0].start()
 
     def start_late_pair():
         carry_copy.start()
         part_copies[1].start()
+
+    @pl.when(half == 1)
+    def _():
+        hello_copy.start()
 
     @pl.when(core == 1)
     def _():
@@ -349,6 +352,7 @@
     @pl.when(half == 0)
     def _():
         pl.semaphore_wait(ready, 1)
+        hello_copy.start()
         start_pair()
 
     @pl.when(half == 1)
@@ -379,10 +383,6 @@
     rank_in[head] = rank_out[head]
     send_plane(0, lambda peer: rank_out.at[peer], lambda slot: rank_in.at[slot])
 
-    @pl.when(half == 0)
-    def _():
-        start_late_pair()
-
     for name, i, buffer, copy in (("hello", 0, hello, hello_copy), ("carry", 1, carry, carry_copy)):
         arriving[name] = pair_copy(i, buffer.at[1 - half], buffer.at[1 - half]).wait_recv
         leaving[name] = copy.wait_send
@@ -452,6 +452,11 @@
 
     make_maps(0)
     send_maps(0)
+
+    @pl.when(half == 0)
+    def _():
+        start_late_pair()
+
     make_maps(1)
     send_maps(1)
 

time: 50.8 us -> 50.4 us (level)
  the two profiles are of different devices: /device:TPU:448 before, /device:TPU:160 now
where the time goes in v6:
time: 50.4 us; the launch traced here: 50.2 us
  Pallas kernels  47.4 us (94%)
  local copies, waits for them, and re-layouts  1.47 us (3%)
  between operations  1.29 us (3%)
    pallas_call x1, Pallas kernels, run(): pl.pallas_call(functools.partial(kernel, groups, heads), out_shape=jax.Sh...  47.4 us
    slice x1, local copies, waits for them, and re-layouts, run(): return (result[:, :, :C], result[:, :, C:])  1.47 us

profile of v6, /device:TPU:160, one launch (start us, length us, event | category | flops | bytes accessed | tf_op | source)
XLA Modules:
  0.0 50.2 jit_solution(14291862539102888188)
XLA Ops:
  1.3 47.4 %shard_map.113 = f32[1,32,128]{2,1,0:T(8,128)} custom-call(s32[1]{0:T(128)S(6)} %copy.12.start_ref, f32[1,32,64]{2,1,0:T(8,128)} %latent_hbm.1, f32[1,2,32,64]{3,2,1,0:T(8,128)} %noise_hbm.1, f32[10,6144]{1,0:T(8,128)} %mod_hbm.1, bf16[64,3072]{1,0:T(8,128)(2,1)} %win_hbm.1, f32[1,3072]{1,0:T(1,128)} %bitcast.2, bf16[3,1,1536,128]{3,2,1,0:T(8,128)(2,1)} %base_hbm.1, ...), custom_call_target="tpu_custom_call" | custom-call | tf_op jit(solution)/shard_map/pallas_call | solution.py:532
  48.7 1.5 %fusion = (f32[1,32,64]{2,1,0:T(8,128)}, f32[1,32,64]{2,1,0:T(8,128)}) fusion(f32[1,32,128]{2,1,0:T(8,128)} %shard_map.113), kind=kLoop, calls=%fused_computation | loop fusion | bytes 32768 | tf_op jit(solution)/shard_map/slice | solution.py:583

commit v7 on v6

--- a/solution.py
+++ b/solution.py
@@ -278,8 +278,8 @@
         part_copies[0].start()
 
     def start_late_pair():
+        part_copies[1].start()
         carry_copy.start()
-        part_copies[1].start()
 
     @pl.when(half == 1)
     def _():

time: 50.4 us -> 49.8 us (0.988)
  Pallas kernels: 47.4 us -> 46.8 us
    pallas_call x1, Pallas kernels: 47.4 us -> 46.8 us  [run(): pl.pallas_call(functools.partial(kernel, groups, heads), out_shape=jax.Sh...]
where the time goes in v7:
time: 49.8 us; the launch traced here: 49.6 us
  Pallas kernels  46.8 us (94%)
  local copies, waits for them, and re-layouts  1.47 us (3%)
  between operations  1.29 us (3%)
    pallas_call x1, Pallas kernels, run(): pl.pallas_call(functools.partial(kernel, groups, heads), out_shape=jax.Sh...  46.8 us
    slice x1, local copies, waits for them, and re-layouts, run(): return (result[:, :, :C], result[:, :, C:])  1.47 us

profile of v7, /device:TPU:160, one launch (start us, length us, event | category | flops | bytes accessed | tf_op | source)
XLA Modules:
  0.0 49.6 jit_solution(10249097978712377915)
XLA Ops:
  1.3 46.8 %shard_map.113 = f32[1,32,128]{2,1,0:T(8,128)} custom-call(s32[1]{0:T(128)S(6)} %copy.12.start_ref, f32[1,32,64]{2,1,0:T(8,128)} %latent_hbm.1, f32[1,2,32,64]{3,2,1,0:T(8,128)} %noise_hbm.1, f32[10,6144]{1,0:T(8,128)} %mod_hbm.1, bf16[64,3072]{1,0:T(8,128)(2,1)} %win_hbm.1, f32[1,3072]{1,0:T(1,128)} %bitcast.2, bf16[3,1,1536,128]{3,2,1,0:T(8,128)(2,1)} %base_hbm.1, ...), custom_call_target="tpu_custom_call" | custom-call | tf_op jit(solution)/shard_map/pallas_call | solution.py:532
  48.1 1.5 %fusion = (f32[1,32,64]{2,1,0:T(8,128)}, f32[1,32,64]{2,1,0:T(8,128)}) fusion(f32[1,32,128]{2,1,0:T(8,128)} %shard_map.113), kind=kLoop, calls=%fused_computation | loop fusion | bytes 32768 | tf_op jit(solution)/shard_map/slice | solution.py:583
